TPU v7x, 32 devices: a whole 2x2x4 slice. The times are simulated.
32 devices in a mesh: fsdp: 8 (over y, x, core), seq: 4 (over z).
Axes of the slice: x: 2, y: 2, z: 4, core: 2. Of those that a mesh axis runs over, the one named last changes fastest.
Arguments:
- tokens: bfloat16 [16, 1376, 1024], P('fsdp', 'seq'), may hold values from -24 to 24
- valid_len: int32 [16], P('fsdp'), may hold values from 1204 to 1376, as said below
- cotangent: bfloat16 [16, 1376, 1024], P('fsdp', 'seq'), may hold values from -6 to 6
- norm1_gain: bfloat16 [1024], P('fsdp'), may hold values from 0.59765625 to 1.3984375
- norm1_shift: bfloat16 [1024], P('fsdp'), may hold values from -1 to 1
- qkv_weight: bfloat16 [1024, 3072], P('fsdp'), may hold values from -0.1875 to 0.1875
- query_bias: bfloat16 [1024], P('fsdp'), may hold values from -1.5 to 1.5
- value_bias: bfloat16 [1024], P('fsdp'), may hold values from -0.29882812 to 0.29882812
- proj_weight: bfloat16 [1024, 1024], P('fsdp'), may hold values from -3 to 3
- proj_bias: bfloat16 [1024], P('fsdp'), may hold values from -1 to 1
- attn_scale: bfloat16 [1024], P('fsdp'), may hold values from 0.5 to 1.5
- norm2_gain: bfloat16 [1024], P('fsdp'), may hold values from 0.59765625 to 1.3984375
- norm2_shift: bfloat16 [1024], P('fsdp'), may hold values from -1 to 1
- fc1_weight: bfloat16 [1024, 4096], P('fsdp'), may hold values from -0.1875 to 0.1875
- fc1_bias: bfloat16 [4096], P('fsdp'), may hold values from -1.5 to 1.5
- fc2_weight: bfloat16 [4096, 1024], P('fsdp'), may hold values from -0.125 to 0.125
- fc2_bias: bfloat16 [1024], P('fsdp'), may hold values from -1 to 1
- mlp_scale: bfloat16 [1024], P('fsdp'), may hold values from 0.5 to 1.5
Outputs:
- mixed: bfloat16 [16, 1376, 1024], P('fsdp', 'seq')
- input_grad: float32 [16, 1376, 1024], P('fsdp', 'seq')
- rms_stats: float32 [16, 5], P('fsdp')
- grad_norm1_gain: float32 [1024], P('fsdp')
- grad_norm1_shift: float32 [1024], P('fsdp')
- grad_qkv_weight: float32 [1024, 3072], P('fsdp')
- grad_query_bias: float32 [1024], P('fsdp')
- grad_value_bias: float32 [1024], P('fsdp')
- grad_proj_weight: float32 [1024, 1024], P('fsdp')
- grad_proj_bias: float32 [1024], P('fsdp')
- grad_attn_scale: float32 [1024], P('fsdp')
- grad_norm2_gain: float32 [1024], P('fsdp')
- grad_norm2_shift: float32 [1024], P('fsdp')
- grad_fc1_weight: float32 [1024, 4096], P('fsdp')
- grad_fc1_bias: float32 [4096], P('fsdp')
- grad_fc2_weight: float32 [4096, 1024], P('fsdp')
- grad_fc2_bias: float32 [1024], P('fsdp')
- grad_mlp_scale: float32 [1024], P('fsdp')
Inputs may be any that keep to these rules, and one draw needn't show every extreme that they name: Token slots at or above an image's valid_len are padding; some image has 1376 and some has 1204 in every draw.
All inputs are finite; a program needn't handle non-finite values.
Results may differ from a plain program's by a relative error of at most 0.01.
Values may be sent and summed in bfloat16 or wider, within the bound.
A program may use at most 256 MiB of HBM per device.

v0:
```python
import jax
import jax.numpy as jnp
from jax import lax
from jax.sharding import PartitionSpec as P

HEAD_DIM = 64


EPSILON = 1e-06


def for_sending(value):
    return jax.tree.map(lambda a: a.astype(jnp.bfloat16) if a.dtype == jnp.float32 else a, value)


def layer_norm(values, gain, shift):
    average = jnp.mean(values, axis=-1, keepdims=True)
    centered = values - average
    variance = jnp.mean(centered * centered, axis=-1, keepdims=True)
    return centered * lax.rsqrt(variance + EPSILON) * gain + shift


def gelu_exact(values):
    return jax.nn.gelu(values, approximate=False)


def block_rows(length):
    return length // 2


def attend_image(inputs_one):
    queries, keys_in, values_in, length_one = inputs_one
    length = queries.shape[0]
    rows = block_rows(length)
    scaling = queries.shape[2] ** (-0.5)
    live_keys = (jnp.arange(length, dtype=jnp.int32) < length_one)[None, None, :]
    outputs = []
    totals = []
    for section in range(length // rows):
        part_q = queries[section * rows : (section + 1) * rows]
        scores = (
            jnp.einsum("qhe,khe->hqk", part_q, keys_in, preferred_element_type=jnp.float32)
            * scaling
        )
        scores = jnp.where(live_keys, scores, -1e30)
        highest = jnp.max(scores, axis=-1, keepdims=True)
        exponent = jnp.exp(scores - highest)
        row_sums = jnp.sum(exponent, axis=-1, keepdims=True)
        probabilities = (exponent / row_sums).astype(jnp.bfloat16)
        outputs.append(
            jnp.einsum("hqk,khe->qhe", probabilities, values_in, preferred_element_type=jnp.float32)
        )
        totals.append(highest + jnp.log(row_sums))
    return (jnp.concatenate(outputs, axis=0).astype(jnp.bfloat16), jnp.concatenate(totals, axis=1))


def attend_back(inputs_one):
    queries, keys_in, values_in, grad_out, log_total, length_one = inputs_one
    length = queries.shape[0]
    rows = block_rows(length)
    scaling = queries.shape[2] ** (-0.5)
    live_keys = (jnp.arange(length, dtype=jnp.int32) < length_one)[None, None, :]
    grad_keys = jnp.zeros(keys_in.shape, jnp.float32)
    grad_values = jnp.zeros(values_in.shape, jnp.float32)
    grad_queries = []
    for section in range(length // rows):
        part_q = queries[section * rows : (section + 1) * rows]
        part_grad = grad_out[section * rows : (section + 1) * rows]
        part_total = log_total[:, section * rows : (section + 1) * rows]
        scores = (
            jnp.einsum("qhe,khe->hqk", part_q, keys_in, preferred_element_type=jnp.float32)
            * scaling
        )
        scores = jnp.where(live_keys, scores, -1e30)
        probabilities = jnp.exp(scores - part_total)
        rounded = probabilities.astype(jnp.bfloat16)
        grad_prob = jnp.einsum(
            "qhe,khe->hqk", part_grad, values_in, preferred_element_type=jnp.float32
        )
        centre = jnp.sum(probabilities * grad_prob, axis=-1, keepdims=True)
        grad_scores = (probabilities * (grad_prob - centre)).astype(jnp.bfloat16)
        grad_queries.append(
            jnp.einsum("hqk,khe->qhe", grad_scores, keys_in, preferred_element_type=jnp.float32)
            * scaling
        )
        grad_keys = (
            grad_keys
            + jnp.einsum("hqk,qhe->khe", grad_scores, part_q, preferred_element_type=jnp.float32)
            * scaling
        )
        grad_values = grad_values + jnp.einsum(
            "hqk,qhe->khe", rounded, part_grad, preferred_element_type=jnp.float32
        )
    stacked = jnp.stack([jnp.concatenate(grad_queries, axis=0), grad_keys, grad_values], axis=1)
    return stacked.astype(jnp.bfloat16)


def per_device(
    tokens,
    valid_len,
    cotangent,
    norm1_gain,
    norm1_shift,
    qkv_weight,
    query_bias,
    value_bias,
    proj_weight,
    proj_bias,
    attn_scale,
    norm2_gain,
    norm2_shift,
    fc1_weight,
    fc1_bias,
    fc2_weight,
    fc2_bias,
    mlp_scale,
):
    gathered = (
        lax.all_gather(norm1_gain, "fsdp", axis=0, tiled=True),
        lax.all_gather(norm1_shift, "fsdp", axis=0, tiled=True),
        lax.all_gather(qkv_weight, "fsdp", axis=0, tiled=True),
        lax.all_gather(query_bias, "fsdp", axis=0, tiled=True),
        lax.all_gather(value_bias, "fsdp", axis=0, tiled=True),
        lax.all_gather(proj_weight, "fsdp", axis=0, tiled=True),
        lax.all_gather(proj_bias, "fsdp", axis=0, tiled=True),
        lax.all_gather(attn_scale, "fsdp", axis=0, tiled=True),
        lax.all_gather(norm2_gain, "fsdp", axis=0, tiled=True),
        lax.all_gather(norm2_shift, "fsdp", axis=0, tiled=True),
        lax.all_gather(fc1_weight, "fsdp", axis=0, tiled=True),
        lax.all_gather(fc1_bias, "fsdp", axis=0, tiled=True),
        lax.all_gather(fc2_weight, "fsdp", axis=0, tiled=True),
        lax.all_gather(fc2_bias, "fsdp", axis=0, tiled=True),
        lax.all_gather(mlp_scale, "fsdp", axis=0, tiled=True),
    )
    (
        gain_one,
        shift_one,
        weight_qkv,
        bias_query,
        bias_value,
        weight_proj,
        bias_proj,
        scale_one,
        gain_two,
        shift_two,
        weight_up,
        bias_up,
        weight_down,
        bias_down,
        scale_two,
    ) = gathered
    images_here, tok_here, width = tokens.shape
    seq_count = lax.axis_size("seq")
    head_cols = width // seq_count
    heads_here = head_cols // HEAD_DIM
    length = tok_here * seq_count
    inputs_f = tokens.astype(jnp.float32)
    gain_first = gain_one.astype(jnp.float32)
    shift_first = shift_one.astype(jnp.float32)
    gain_second = gain_two.astype(jnp.float32)
    shift_second = shift_two.astype(jnp.float32)
    scale_first = scale_one.astype(jnp.float32)
    scale_second = scale_two.astype(jnp.float32)
    normed_first = layer_norm(inputs_f, gain_first, shift_first).astype(jnp.bfloat16)
    bias_all = jnp.concatenate(
        [
            bias_query.astype(jnp.float32),
            jnp.zeros((width,), jnp.float32),
            bias_value.astype(jnp.float32),
        ]
    )
    projected = (
        jnp.einsum("mtd,de->mte", normed_first, weight_qkv, preferred_element_type=jnp.float32)
        + bias_all
    ).astype(jnp.bfloat16)
    by_heads = lax.all_to_all(
        projected.reshape(images_here, tok_here, 3, seq_count, head_cols),
        "seq",
        split_axis=3,
        concat_axis=1,
        tiled=True,
    )
    by_heads = by_heads.reshape(images_here, length, 3, heads_here, HEAD_DIM)
    attended, log_total = lax.map(
        attend_image, (by_heads[:, :, 0], by_heads[:, :, 1], by_heads[:, :, 2], valid_len)
    )
    attended_tok = lax.all_to_all(
        for_sending(attended.reshape(images_here, length, 1, head_cols)),
        "seq",
        split_axis=1,
        concat_axis=2,
        tiled=True,
    )
    attended_tok = attended_tok.reshape(images_here, tok_here, width)
    attn_out = jnp.einsum(
        "mtd,de->mte", attended_tok, weight_proj, preferred_element_type=jnp.float32
    ) + bias_proj.astype(jnp.float32)
    branch_attn = scale_first * attn_out
    middle = inputs_f + branch_attn
    normed_second = layer_norm(middle, gain_second, shift_second).astype(jnp.bfloat16)
    hidden_pre = jnp.einsum(
        "mtd,df->mtf", normed_second, weight_up, preferred_element_type=jnp.float32
    ) + bias_up.astype(jnp.float32)
    hidden = gelu_exact(hidden_pre).astype(jnp.bfloat16)
    mlp_out = jnp.einsum(
        "mtf,fd->mtd", hidden, weight_down, preferred_element_type=jnp.float32
    ) + bias_down.astype(jnp.float32)
    branch_mlp = scale_second * mlp_out
    result = middle + branch_mlp
    positions = lax.axis_index("seq") * tok_here + jnp.arange(tok_here, dtype=jnp.int32)
    live = (positions[None, :] < valid_len[:, None]).astype(jnp.float32)[:, :, None]
    squares = jnp.stack(
        [
            jnp.sum(live * piece * piece, axis=(1, 2))
            for piece in (inputs_f, branch_attn, middle, branch_mlp, result)
        ],
        axis=-1,
    )
    squares = lax.psum(squares, "seq")
    rms_stats = jnp.sqrt(squares / (valid_len.astype(jnp.float32)[:, None] * width))
    grad_result = cotangent.astype(jnp.float32)
    grad_mlp_scale = jnp.sum(grad_result * mlp_out, axis=(0, 1))
    grad_mlp_out = (grad_result * scale_second).astype(jnp.bfloat16)
    grad_fc2_bias = jnp.sum(grad_mlp_out, axis=(0, 1), dtype=jnp.float32)
    grad_fc2_weight = jnp.einsum(
        "mtf,mtd->fd", hidden, grad_mlp_out, preferred_element_type=jnp.float32
    )
    grad_hidden = jnp.einsum(
        "mtd,fd->mtf", grad_mlp_out, weight_down, preferred_element_type=jnp.float32
    )
    gelu_value, gelu_back = jax.vjp(gelu_exact, hidden_pre)
    grad_pre = gelu_back(grad_hidden)[0].astype(jnp.bfloat16)
    grad_fc1_bias = jnp.sum(grad_pre, axis=(0, 1), dtype=jnp.float32)
    grad_fc1_weight = jnp.einsum(
        "mtd,mtf->df", normed_second, grad_pre, preferred_element_type=jnp.float32
    )
    grad_normed_second = jnp.einsum(
        "mtf,df->mtd", grad_pre, weight_up, preferred_element_type=jnp.float32
    )
    norm_value, norm_back = jax.vjp(layer_norm, middle, gain_second, shift_second)
    grad_middle_norm, grad_norm2_gain, grad_norm2_shift = norm_back(grad_normed_second)
    grad_middle = grad_result + grad_middle_norm
    grad_attn_scale = jnp.sum(grad_middle * attn_out, axis=(0, 1))
    grad_attn_out = (grad_middle * scale_first).astype(jnp.bfloat16)
    grad_proj_bias = jnp.sum(grad_attn_out, axis=(0, 1), dtype=jnp.float32)
    grad_proj_weight = jnp.einsum(
        "mtd,mte->de", attended_tok, grad_attn_out, preferred_element_type=jnp.float32
    )
    grad_attended = jnp.einsum(
        "mte,de->mtd", grad_attn_out, weight_proj, preferred_element_type=jnp.float32
    ).astype(jnp.bfloat16)
    grad_heads = lax.all_to_all(
        grad_attended.reshape(images_here, tok_here, seq_count, head_cols),
        "seq",
        split_axis=2,
        concat_axis=1,
        tiled=True,
    )
    grad_heads = grad_heads.reshape(images_here, length, heads_here, HEAD_DIM)
    grad_qkv = lax.map(
        attend_back,
        (by_heads[:, :, 0], by_heads[:, :, 1], by_heads[:, :, 2], grad_heads, log_total, valid_len),
    )
    grad_projected = lax.all_to_all(
        for_sending(grad_qkv.reshape(images_here, length, 3, 1, head_cols)),
        "seq",
        split_axis=1,
        concat_axis=3,
        tiled=True,
    )
    grad_projected = grad_projected.reshape(images_here, tok_here, 3 * width)
    grad_query_bias = jnp.sum(grad_projected[:, :, :width], axis=(0, 1), dtype=jnp.float32)
    grad_value_bias = jnp.sum(grad_projected[:, :, 2 * width :], axis=(0, 1), dtype=jnp.float32)
    grad_qkv_weight = jnp.einsum(
        "mtd,mte->de", normed_first, grad_projected, preferred_element_type=jnp.float32
    )
    grad_normed_first = jnp.einsum(
        "mte,de->mtd", grad_projected, weight_qkv, preferred_element_type=jnp.float32
    )
    first_value, first_back = jax.vjp(layer_norm, inputs_f, gain_first, shift_first)
    grad_input_norm, grad_norm1_gain, grad_norm1_shift = first_back(grad_normed_first)
    input_grad = grad_middle + grad_input_norm
    reduced = (
        lax.psum_scatter(grad_norm1_gain, "fsdp", scatter_dimension=0, tiled=True),
        lax.psum_scatter(grad_norm1_shift, "fsdp", scatter_dimension=0, tiled=True),
        lax.psum_scatter(grad_qkv_weight, "fsdp", scatter_dimension=0, tiled=True),
        lax.psum_scatter(grad_query_bias, "fsdp", scatter_dimension=0, tiled=True),
        lax.psum_scatter(grad_value_bias, "fsdp", scatter_dimension=0, tiled=True),
        lax.psum_scatter(grad_proj_weight, "fsdp", scatter_dimension=0, tiled=True),
        lax.psum_scatter(grad_proj_bias, "fsdp", scatter_dimension=0, tiled=True),
        lax.psum_scatter(grad_attn_scale, "fsdp", scatter_dimension=0, tiled=True),
        lax.psum_scatter(grad_norm2_gain, "fsdp", scatter_dimension=0, tiled=True),
        lax.psum_scatter(grad_norm2_shift, "fsdp", scatter_dimension=0, tiled=True),
        lax.psum_scatter(grad_fc1_weight, "fsdp", scatter_dimension=0, tiled=True),
        lax.psum_scatter(grad_fc1_bias, "fsdp", scatter_dimension=0, tiled=True),
        lax.psum_scatter(grad_fc2_weight, "fsdp", scatter_dimension=0, tiled=True),
        lax.psum_scatter(grad_fc2_bias, "fsdp", scatter_dimension=0, tiled=True),
        lax.psum_scatter(grad_mlp_scale, "fsdp", scatter_dimension=0, tiled=True),
    )
    reduced = lax.psum(
        (
            reduced[0],
            reduced[1],
            reduced[2],
            reduced[3],
            reduced[4],
            reduced[5],
            reduced[6],
            reduced[7],
            reduced[8],
            reduced[9],
            reduced[10],
            reduced[11],
            reduced[12],
            reduced[13],
            reduced[14],
        ),
        "seq",
    )
    return (
        result.astype(jnp.bfloat16),
        input_grad,
        rms_stats,
        reduced[0],
        reduced[1],
        reduced[2],
        reduced[3],
        reduced[4],
        reduced[5],
        reduced[6],
        reduced[7],
        reduced[8],
        reduced[9],
        reduced[10],
        reduced[11],
        reduced[12],
        reduced[13],
        reduced[14],
    )


def solution(mesh):
    in_specs = (
        P("fsdp", "seq", None),
        P("fsdp"),
        P("fsdp", "seq", None),
        P("fsdp"),
        P("fsdp"),
        P("fsdp", None),
        P("fsdp"),
        P("fsdp"),
        P("fsdp", None),
        P("fsdp"),
        P("fsdp"),
        P("fsdp"),
        P("fsdp"),
        P("fsdp", None),
        P("fsdp"),
        P("fsdp", None),
        P("fsdp"),
        P("fsdp"),
    )
    out_specs = (
        P("fsdp", "seq", None),
        P("fsdp", "seq", None),
        P("fsdp", None),
        P("fsdp"),
        P("fsdp"),
        P("fsdp", None),
        P("fsdp"),
        P("fsdp"),
        P("fsdp", None),
        P("fsdp"),
        P("fsdp"),
        P("fsdp"),
        P("fsdp"),
        P("fsdp", None),
        P("fsdp"),
        P("fsdp", None),
        P("fsdp"),
        P("fsdp"),
    )
    return jax.shard_map(
        per_device, mesh=mesh, in_specs=in_specs, out_specs=out_specs, check_vma=False
    )
```

profile of v0, /device:TPU:0, one launch (start us, length us, event | category | flops | bytes accessed | tf_op | source)
XLA Modules:
  0.0 1183.4 jit_solution(1111811643826946012)
XLA Ops:
  86.3 94.0 %all-to-all-done = bf16[2,344,3,4,256]{4,1,2,0,3:T(8,128)(2,1)} async-done(((bf16[2,344,3,4,256]{4,1,2,0,3:T(8,128)(2,1)}), bf16[2,344,3,4,256]{4,1,2,0,3:T(8,128)(2,1)}, u32[]{:S(2)}, u32[]{:S(2)}) %all-to-all-start) | async-done | bytes 4227104 | tf_op jit(solution)/shard_map/all_to_all | solution.py:176
  201.1 86.3 %while.22 = (s32[]{:T(128)}, bf16[2,1376,4,64]{1,3,2,0:T(8,128)(2,1)}, f32[2,4,1376,1]{2,1,3,0:T(4,128)S(1)}, bf16[2,1376,4,64]{1,3,2,0:T(8,128)(2,1)}, s32[2]{0...) while((s32[]{:T(128)}, ...), condition=%wide.region_7.8_spmd, body=%wide.region_2.7_spmd.sunk | while | flops 2031461632 | bytes 149763792 | solution.py:184
  210.3 12.9 %fusion.178 = (f32[4,688]{1,0:T(4,128)S(1)}, f32[4,688]{1,0:T(4,128)S(1)}, f32[4,688,1376]{2,1,0:T(8,128)}) fusion(f32[4,688,1376]{2,1,0:T(8,128)} %get-tuple-element.362, f32[4,688]{1,0:T(4,128)S(1)} %get-tuple-element.363, pred[1376]{0:T(1024)(128)(4,1)S(1)} %iota_compare_fusion.4, bf16[2,1376,4,64]{1,3,2,0:T(8,128)(2,1)S(1)} %get-tuple-element.409, ...), kind=kOutput, calls=%fused_computation.8.clone.1 | convolution fusion | flops 511206016 | bytes 31797764 | tf_op jit(solution)/shard_map/while/body/eval_jaxpr/qhe,khe->hqk/dot_general | solution.py:42
  253.4 12.9 %fusion.178 = (f32[4,688]{1,0:T(4,128)S(1)}, f32[4,688]{1,0:T(4,128)S(1)}, f32[4,688,1376]{2,1,0:T(8,128)}) fusion(f32[4,688,1376]{2,1,0:T(8,128)} %get-tuple-element.362, f32[4,688]{1,0:T(4,128)S(1)} %get-tuple-element.363, pred[1376]{0:T(1024)(128)(4,1)S(1)} %iota_compare_fusion.4, bf16[2,1376,4,64]{1,3,2,0:T(8,128)(2,1)S(1)} %get-tuple-element.409, ...), kind=kOutput, calls=%fused_computation.8.clone.1 | convolution fusion | flops 511206016 | bytes 31797764 | tf_op jit(solution)/shard_map/while/body/eval_jaxpr/qhe,khe->hqk/dot_general | solution.py:42
  370.2 16.9 %fusion.115 = (u8[344,4096]{1,0:T(8,128)(4,1)S(1)}, u8[344,4096]{1,0:T(8,128)(4,1)S(1)}, f32[2,344,4096]{2,1,0:T(8,128)}) fusion(f32[4096]{0:T(1024)S(1)} %bitcast.312, bf16[1024,4096]{1,0:T(8,128)(2,1)} %all-gather.20.cloned.1.call-done, f32[2,344,1024]{2,1,0:T(8,128)} %copy-done.7, f32[1024]{0:T(1024)S(1)} %bitcast.310, f32[1024]{0:T(1024)S(1)} %bitcast.304, ...), kind=kOutput, calls=%fused_computation.182 | convolution fusion | flops 5811519488 | bytes 25326976 | tf_op jit(solution)/shard_map/mtd,df->mtf/dot_general | solution.py:201
  387.1 28.7 %multiply_convert_fusion.2 = (bf16[2,344,4096]{2,1,0:T(8,128)(2,1)}, f32[2,344,4096]{2,1,0:T(8,128)}) fusion(f32[2,344,4096]{2,1,0:T(8,128)} %get-tuple-element.261, f32[4096]{0:T(1024)S(1)} %bitcast.313, u8[344,4096]{1,0:T(8,128)(4,1)S(1)} %get-tuple-element.158, u8[344,4096]{1,0:T(8,128)(4,1)S(1)} %get-tuple-element.157), kind=kLoop, calls=%fused_computation.109 | loop fusion | flops 200081408 | bytes 31014912 | tf_op jit(solution)/shard_map/convert_element_type | solution.py:204
  415.9 19.7 %convert_reduce_fusion = (f32[4096]{0:T(1024)}, bf16[2,344,4096]{2,1,0:T(8,128)(2,1)}) fusion(f32[2,344,4096]{2,1,0:T(8,128)} %get-tuple-element.240, bf16[4096,1024]{1,0:T(8,128)(2,1)} %all-gather.22.cloned.1.call-done, bf16[2,344,1024]{2,1,0:T(8,128)(2,1)} %param.24, f32[1024]{0:T(1024)S(1)} %bitcast.321, f32[2,344,4096]{2,1,0:T(8,128)} %get-tuple-element.261, ...), kind=kOutput, calls=%fused_computation.107 | convolution fusion | flops 5821378560 | bytes 38014976 | tf_op jit(solution)/shard_map/mtd,fd->mtf/dot_general | solution.py:228
  445.9 12.0 %fusion.110 = (f32[2]{0:T(128)}, f32[2]{0:T(128)}, f32[1024]{0:T(1024)}, f32[2]{0:T(128)}, f32[2,344]{1,0:T(2,128)S(1)}, /*index=5*/f32[1024]{0:T(1024)}, f32[10...) fusion(f32[2,344]{1,0:T(2,128)S(1)} %compare_convert_fusion, f32[2,344,1024]{2,1,0:T(8,128)S(1)} %copy-done.8, ...), kind=kOutput, calls=%fused_computation.166 | convolution fusion | flops 5791084032 | bytes 22518552 | tf_op jit(solution)/shard_map/mtf,fd->mtd/dot_general | solution.py:205
  467.0 13.9 %convolution_bitcast_fusion.1 = f32[1024,4096]{1,0:T(8,128)} fusion(bf16[2,344,4096]{2,1,0:T(8,128)(2,1)} %get-tuple-element.264, f32[2,344,1024]{2,1,0:T(8,128)} %copy-done.7, f32[1024]{0:T(1024)S(1)} %bitcast.311, f32[1024]{0:T(1024)S(1)} %bitcast.307, f32[2,344]{1,0:T(2,128)S(1)} %fusion.130, f32[2,344]{1,0:T(2,128)S(1)} %broadcast_multiply_fusion), kind=kOutput, calls=%fused_computation.123 | convolution fusion | flops 5774884864 | bytes 25245056 | tf_op jit(solution)/shard_map/mtd,mtf->df/dot_general | solution.py:234
  490.9 12.4 %convolution_bitcast_fusion = f32[4096,1024]{1,0:T(8,128)} fusion(bf16[2,344,4096]{2,1,0:T(8,128)(2,1)} %get-tuple-element.239, bf16[2,344,1024]{2,1,0:T(8,128)(2,1)} %param.24, f32[1024]{0:T(1024)S(1)} %bitcast.323), kind=kOutput, calls=%fused_computation.122 | convolution fusion | flops 5773475840 | bytes 23826432 | tf_op jit(solution)/shard_map/mtf,mtd->fd/dot_general | solution.py:225
  503.3 21.6 %all-to-all-done.2 = bf16[2,344,4,256]{3,1,0,2:T(8,128)(2,1)} async-done(((bf16[2,344,4,256]{3,1,0,2:T(8,128)(2,1)}), bf16[2,344,4,256]{3,1,0,2:T(8,128)(2,1)}, u32[]{:S(2)}, u32[]{:S(2)}) %all-to-all-start.2) | async-done | bytes 1409056 | tf_op jit(solution)/shard_map/all_to_all | solution.py:252
  532.5 184.1 %while.23 = (s32[]{:T(128)}, bf16[2,1376,3,4,64]{1,4,3,2,0:T(8,128)(2,1)}, bf16[2,1376,4,64]{1,3,2,0:T(8,128)(2,1)S(1)}, s32[2]{0:T(128)S(1)}, bf16[2,1376,4,64]...) while((s32[]{:T(128)}, ...), condition=%wide.region_15.16_spmd, body=%wide.region_12.15_spmd.sunk | while | flops 4925415424 | bytes 314920288 | solution.py:260
  532.6 12.0 %fusion.193 = f32[4,688,1376]{2,1,0:T(8,128)} fusion(bf16[2,1376,4,64]{1,3,2,0:T(8,128)(2,1)} %get-tuple-element.442, s32[]{:T(128)} %get-tuple-element.424, bf16[2,1376,4,64]{1,3,2,0:T(8,128)(2,1)} %get-tuple-element.441, s32[]{:T(128)S(6)} %add.371), kind=kOutput, calls=%fused_computation.67.clone.1 | convolution fusion | flops 484704256 | bytes 16262148 | tf_op jit(solution)/shard_map/while/body/eval_jaxpr/qhe,khe->hqk/dot_general | solution.py:77
  574.8 11.5 multiply_reduce_fusion.9
  586.2 14.9 %multiply_convert_fusion.7 = bf16[4,688,1376]{2,1,0:T(8,128)(2,1)} fusion(f32[4,688,1376]{2,1,0:T(8,128)} %get-tuple-element.380, f32[4,688,1376]{2,1,0:T(8,128)} %fusion.195, f32[4,688]{1,0:T(4,128)S(1)} %get-tuple-element.381), kind=kLoop, calls=%fused_computation.45.clone.1 | loop fusion | flops 11360256 | bytes 37878528 | tf_op jit(solution)/shard_map/while/body/eval_jaxpr/convert_element_type | solution.py:81
  654.8 11.6 fusion.195
  666.4 12.0 %multiply_reduce_fusion.9 = (f32[4,688]{1,0:T(4,128)S(1)}, f32[4,688,1376]{2,1,0:T(8,128)}) fusion(f32[4,688,1376]{2,1,0:T(8,128)} %fusion.195, f32[4,688]{1,0:T(4,128)S(1)} %get-tuple-element.379, bf16[2,1376,4,64]{1,3,2,0:T(8,128)(2,1)S(1)} %get-tuple-element.437, s32[]{:T(128)} %get-tuple-element.424, ...), kind=kOutput, calls=%fused_computation.46.clone.1 | convolution fusion | flops 503635264 | bytes 31786752 | tf_op jit(solution)/shard_map/while/body/eval_jaxpr/qhe,khe->hqk/dot_general | solution.py:71
  678.4 14.8 %multiply_convert_fusion.7 = bf16[4,688,1376]{2,1,0:T(8,128)(2,1)} fusion(f32[4,688,1376]{2,1,0:T(8,128)} %get-tuple-element.380, f32[4,688,1376]{2,1,0:T(8,128)} %fusion.195, f32[4,688]{1,0:T(4,128)S(1)} %get-tuple-element.381), kind=kLoop, calls=%fused_computation.45.clone.1 | loop fusion | flops 11360256 | bytes 37878528 | tf_op jit(solution)/shard_map/while/body/eval_jaxpr/convert_element_type | solution.py:81
  716.6 12.5 %copy.60 = bf16[2,1376,3,1,256]{4,0,3,2,1:T(2,128)(2,1)} copy(bf16[2,1376,3,1,256]{1,4,2,0,3:T(8,128)(2,1)} %bitcast.64) | data formatting | bytes 8454144 | tf_op jit(solution)/shard_map/reshape | solution.py:265
  729.0 97.8 %all_to_all.60 = bf16[2,1376,3,1,256]{4,0,3,2,1:T(2,128)(2,1)S(1)} all-to-all(bf16[2,1376,3,1,256]{4,0,3,2,1:T(2,128)(2,1)} %copy.60), channel_id=1, replica_groups=mesh['fsdp'=8,'seq'=4] {'seq'}, dimensions={1} | all-to-all | bytes 8454144 | tf_op jit(solution)/shard_map/all_to_all | solution.py:264
  850.1 91.9 %reduce-scatter.5.cloned.1.call-done = f32[128,3072]{1,0:T(8,128)} async-done(((f32[1024,3072]{1,0:T(8,128)}), f32[128,3072]{1,0:T(8,128)}) %reduce-scatter.5.cloned.1.call-update) | async-done | bytes 1572880 | tf_op jit(solution)/shard_map/reduce_scatter | solution.py:286
  957.6 25.2 %all-reduce.11 = (f32[1024]{0:T(1024)S(1)}, f32[1024]{0:T(1024)S(1)}, f32[1024]{0:T(1024)S(1)}, f32[1024]{0:T(1024)S(1)}, f32[1024]{0:T(1024)S(1)}, /*index=5*/f...) all-reduce(f32[1024]{0:T(1024)S(1)} %get-tuple-element.161, ...), channel_id=2, replica_groups=mesh['fsdp'=8,'seq'=4] {'fsdp'}, use_global_device_ids=true, to_apply=%region_25.26.clone | all-reduce | flops 14336 | bytes 114688
  983.8 13.5 %all-reduce.12 = (f32[2,5]{1,0:T(2,128)S(1)}, f32[128]{0:T(128)}, f32[128]{0:T(128)}, f32[128]{0:T(128)}, f32[128]{0:T(128)}, /*index=5*/f32[128]{0:T(128)}, f32...) all-reduce(f32[2,5]{1,0:T(2,128)S(1)} %stack.35, ...), channel_id=1, replica_groups=mesh['fsdp'=8,'seq'=4] {'seq'}, use_global_device_ids=true, to_apply=%region_23.24 | all-reduce | flops 1802 | bytes 14416 | tf_op jit(solution)/shard_map/psum | solution.py:219
  1002.3 167.0 %all-reduce.16.cloned.1.call-done = (f32[128,3072]{1,0:T(8,128)}, f32[128,1024]{1,0:T(8,128)}, f32[128,4096]{1,0:T(8,128)}, f32[512,1024]{1,0:T(8,128)}) async-done(((f32[128,3072]{1,0:T(8,128)}, f32[128,1024]{1,0:T(8,128)}, f32[128,4096]{1,0:T(8,128)}, f32[512,1024]{1,0:T(8,128)}), (f32[128,3072]{1,0:T(8,128)}, f32[128,1024]{1,0:T(8,128)}, f32[128,4096]{1,0:T(8,128)}, ...) | async-done | bytes 6291472 | tf_op jit(solution)/shard_map/psum | solution.py:300
  (325 shorter events, 436.9 us)
Async XLA Ops:
  7.2 51.0 %all-gather.16.cloned.1.call-start = ((), (), s32[]{:S(2)}) async-start(), calls=%async_computation.8 | async-start | bytes 7077888 | tf_op jit(solution)/shard_map/all_gather | solution.py:121
  7.9 354.4 %all-gather.18.cloned.1.call-start = ((), (), s32[]{:S(2)}) async-start(), calls=%async_computation.9 | async-start | bytes 2359296 | tf_op jit(solution)/shard_map/all_gather | solution.py:124
  8.7 361.5 %all-gather.20.cloned.1.call-start = ((), (), s32[]{:S(2)}) async-start(), calls=%async_computation.10 | async-start | bytes 9437184 | tf_op jit(solution)/shard_map/all_gather | solution.py:129
  19.7 47.7 %copy-start.18 = (f32[8,1,128]{2,1,0:T(1,128)}, f32[8,1,128]{2,1,0:T(1,128)S(1)}, u32[]{:S(2)}) copy-start(f32[8,1,128]{2,1,0:T(1,128)S(1)} %convert_element_type.155) | copy-start | bytes 12292
  80.8 99.5 %all-to-all-start = ((bf16[2,344,3,4,256]{4,1,2,0,3:T(8,128)(2,1)}), bf16[2,344,3,4,256]{4,1,2,0,3:T(8,128)(2,1)}, u32[]{:S(2)}, u32[]{:S(2)}) async-start(bf16[2,344,3,4,256]{4,1,2,0,3:T(8,128)(2,1)} %copy.53), calls=%async_computation | async-start | bytes 8454144 | tf_op jit(solution)/shard_map/all_to_all | solution.py:176
  85.7 330.2 %all-gather.22.cloned.1.call-start = ((), (), s32[]{:S(2)}) async-start(), calls=%async_computation.11 | async-start | bytes 9437184 | tf_op jit(solution)/shard_map/all_gather | solution.py:131
  287.5 51.3 %copy-start.47 = (bf16[128]{0:T(256)(128)(2,1)S(1)}, bf16[128]{0:T(256)(128)(2,1)}, u32[]{:S(2)}) copy-start(bf16[128]{0:T(256)(128)(2,1)} %param.39) | copy-start | bytes 772
  287.5 59.1 %copy-start.48 = (bf16[128]{0:T(256)(128)(2,1)S(1)}, bf16[128]{0:T(256)(128)(2,1)}, u32[]{:S(2)}) copy-start(bf16[128]{0:T(256)(128)(2,1)} %param.38) | copy-start | bytes 772
  292.3 63.0 %all-to-all-start.1 = ((bf16[2,1376,1,256]{3,0,2,1:T(2,128)(2,1)}), bf16[2,1376,1,256]{3,0,2,1:T(2,128)(2,1)}, u32[]{:S(2)}, u32[]{:S(2)}) async-start(bf16[2,1376,1,256]{3,0,2,1:T(2,128)(2,1)} %copy.55), calls=%async_computation.1 | async-start | bytes 2818048 | tf_op jit(solution)/shard_map/all_to_all | solution.py:187
  296.7 553.4 %reduce-scatter.7.cloned.1.call-start = ((), (), s32[]{:S(2)}) async-start(), calls=%async_computation.13 | async-start | bytes 4718592 | tf_op jit(solution)/shard_map/reduce_scatter | solution.py:289
  355.4 103.5 %copy-start.35 = (f32[2,344]{1,0:T(2,128)}, f32[2,344]{1,0:T(2,128)S(1)}, u32[]{:S(2)}) copy-start(f32[2,344]{1,0:T(2,128)S(1)} %compare_convert_fusion) | copy-start | bytes 8260
  466.9 383.1 %reduce-scatter.9.cloned.1.call-start = ((), (), s32[]{:S(2)}) async-start(), calls=%async_computation.14 | async-start | bytes 18874368 | tf_op jit(solution)/shard_map/reduce_scatter | solution.py:294
  485.9 39.0 %all-to-all-start.2 = ((bf16[2,344,4,256]{3,1,0,2:T(8,128)(2,1)}), bf16[2,344,4,256]{3,1,0,2:T(8,128)(2,1)}, u32[]{:S(2)}, u32[]{:S(2)}) async-start(bf16[2,344,4,256]{3,1,0,2:T(8,128)(2,1)} %bitcast.296), calls=%async_computation.2 | async-start | bytes 2818048 | tf_op jit(solution)/shard_map/all_to_all | solution.py:252
  490.9 359.2 %reduce-scatter.11.cloned.1.call-start = ((), (), s32[]{:S(2)}) async-start(), calls=%async_computation.15 | async-start | bytes 18874368 | tf_op jit(solution)/shard_map/reduce_scatter | solution.py:296
  503.3 438.8 %reduce-scatter.5.cloned.1.call-start = ((), (), s32[]{:S(2)}) async-start(), calls=%async_computation.12 | async-start | bytes 14155776 | tf_op jit(solution)/shard_map/reduce_scatter | solution.py:286
  849.9 92.2 %copy-start.52 = (u32[32]{0:T(128)S(1)}, u32[32]{0:T(128)}, u32[]{:S(2)}) copy-start(u32[32]{0:T(128)} %constant.139) | copy-start | bytes 388
  849.9 94.1 %copy-start.42 = (f32[2]{0:T(128)S(1)}, f32[2]{0:T(128)}, u32[]{:S(2)}) copy-start(f32[2]{0:T(128)} %get-tuple-element.169) | copy-start | bytes 28
  849.9 94.2 %copy-start.55 = (f32[2]{0:T(128)S(1)}, f32[2]{0:T(128)}, u32[]{:S(2)}) copy-start(f32[2]{0:T(128)} %get-tuple-element.170) | copy-start | bytes 28
  849.9 94.2 %copy-start.54 = (f32[2]{0:T(128)S(1)}, f32[2]{0:T(128)}, u32[]{:S(2)}) copy-start(f32[2]{0:T(128)} %get-tuple-element.166) | copy-start | bytes 28
  850.0 94.3 %copy-start.53 = (f32[2]{0:T(128)S(1)}, f32[2]{0:T(128)}, u32[]{:S(2)}) copy-start(f32[2]{0:T(128)} %get-tuple-element.165) | copy-start | bytes 28
  850.0 94.4 %copy-start.36 = (f32[2,344]{1,0:T(2,128)S(1)}, f32[2,344]{1,0:T(2,128)}, u32[]{:S(2)}) copy-start(f32[2,344]{1,0:T(2,128)} %copy-done.35) | copy-start | bytes 8260
  850.0 319.3 %all-reduce.16.cloned.1.call-start = ((), (), s32[]{:S(2)}) async-start(), calls=%async_computation.16 | async-start | bytes 12582912 | tf_op jit(solution)/shard_map/psum | solution.py:300
  952.7 45.2 %copy-start.12 = (bf16[2,344,1024]{2,1,0:T(8,128)(2,1)S(1)}, bf16[2,344,1024]{2,1,0:T(8,128)(2,1)}, u32[]{:S(2)}) copy-start(bf16[2,344,1024]{2,1,0:T(8,128)(2,1)} %param.24) | copy-start | bytes 4227076
  952.8 45.2 %copy-start.29 = (f32[2,344]{1,0:T(2,128)S(1)}, f32[2,344]{1,0:T(2,128)}, u32[]{:S(2)}) copy-start(f32[2,344]{1,0:T(2,128)} %copy-done.28) | copy-start | bytes 8260
  (64 other events, 656.2 us)
Sparse Core Ops, SparseCore 0:
  9.9 48.2 all-gather.15
  60.1 27.8 all-gather.17
  89.9 54.3 all-gather.19
  146.1 54.3 all-gather.21
  467.1 51.6 reduce-scatter.6
  522.6 115.9 reduce-scatter.8
  642.6 115.9 reduce-scatter.10
  850.0 91.9 reduce-scatter.4
  944.9 224.3 all-reduce.15
where the time goes:
time: 1190 us; the launch traced here: 1180 us
  waiting for transfers between devices  387 us (33%)
  matrix products  322 us (27%)
  blocking collectives  230 us (19%)
  other arithmetic  113 us (9%)
  local copies, waits for them, and re-layouts  99.2 us (8%)
  between operations  16 us (1%)
  starting transfers between devices  15 us (1%)
    psum x1, waiting for transfers between devices, per_device(): lax.psum((reduced[0], reduced[1], reduced[2], reduced[3], reduced[4], red...  167 us
    all_to_all x1, blocking collectives, per_device(): lax.all_to_all(for_sending(grad_qkv.reshape(images_here, length, 3, 1, he...  97.8 us
    all_to_all x1, waiting for transfers between devices, per_device(): lax.all_to_all(projected.reshape(images_here, tok_here, 3, seq_count, hea...  94 us
    reduce_scatter x1, waiting for transfers between devices, per_device(): lax.psum_scatter(grad_qkv_weight, 'fsdp', scatter_dimension=0, tiled=True)  91.9 us
    convert_element_type x4, other arithmetic, attend_back(): grad_scores = (probabilities * (grad_prob - centre)).astype(jnp.bfloat16)  43.6 us
    dot_general x4, matrix products, attend_back(): jnp.einsum('qhe,khe->hqk', part_q, keys_in, preferred_element_type=jnp.fl...  42 us
    dot_general x4, matrix products, attend_back(): jnp.einsum('qhe,khe->hqk', part_grad, values_in, preferred_element_type=j...  41.6 us
    dot_general x4, matrix products, attend_image(): jnp.einsum('qhe,khe->hqk', part_q, keys_in, preferred_element_type=jnp.fl...  41.5 us
  transfers between devices with their start and end apart: 12, of which 5 were waited for; matrix products, arithmetic and copies ran while one was open for 40% of the time, Pallas kernels for 0%

commit v1 on v0

--- a/solution.py
+++ b/solution.py
@@ -1,12 +1,14 @@
+import functools
+
 import jax
 import jax.numpy as jnp
 from jax import lax
+from jax.experimental import pallas as pl
+from jax.experimental.pallas import tpu as pltpu
 from jax.sharding import PartitionSpec as P
 
+EPSILON = 1e-06
 HEAD_DIM = 64
-
-
-EPSILON = 1e-06
 
 
 def for_sending(value):
@@ -95,7 +97,7 @@
     return stacked.astype(jnp.bfloat16)
 
 
-def per_device(
+def generic_device(
     tokens,
     valid_len,
     cotangent,
@@ -339,6 +341,460 @@
     )
 
 
+NT = (((1,), (1,)), ((), ()))
+NN = (((1,), (0,)), ((), ()))
+TN = (((0,), (0,)), ((), ()))
+
+def dotf(a, b, dims):
+    return lax.dot_general(a, b, dims, preferred_element_type=jnp.float32)
+
+def att_fwd_kernel(blocks, q_ref, ko_ref, kp_ref, vo_ref, vp_ref, bias_ref, o_ref, st_ref, kbuf, vbuf):
+    rows = q_ref.shape[0]
+    kbuf[:rows, :128] = ko_ref[...]
+    kbuf[rows:, :128] = kp_ref[...]
+    vbuf[:rows, :128] = vo_ref[...]
+    vbuf[rows:, :128] = vp_ref[...]
+
+    @pl.when(pl.program_id(0) == 0)
+    def _():
+        kbuf[:, 128:] = bias_ref[...]
+        vbuf[:, 128:] = jnp.ones_like(vbuf[:, 128:])
+
+    start = 0
+    for size in blocks:
+        lane = lax.broadcasted_iota(jnp.int32, (size, 128), 1)
+        low = lane < 64
+        first = (lane == 0).astype(jnp.bfloat16)
+        q = q_ref[start:start + size, :]
+        heads = []
+        for h in range(2):
+            keep = low if h == 0 else jnp.logical_not(low)
+            qm = jnp.where(keep, q, jnp.zeros_like(q))
+            qx = jnp.concatenate([qm, first], axis=1)
+            s = dotf(qx, kbuf[...], NT)
+            m = jnp.max(s, axis=-1, keepdims=True)
+            p = jnp.exp(s - m).astype(jnp.bfloat16)
+            ol = dotf(p, vbuf[...], NN)
+            l = ol[:, 128:]
+            heads.append(ol[:, :128] / l)
+            total = -(m + jnp.log(l))
+            hi = total.astype(jnp.bfloat16).astype(jnp.float32)
+            mid = (total - hi).astype(jnp.bfloat16).astype(jnp.float32)
+            lo = total - hi - mid
+            piece = jnp.where(lane == 0, 1.0, jnp.where(lane == 1, hi, jnp.where(lane == 2, mid, jnp.where(lane == 3, lo, 0.0))))
+            st_ref[h, start:start + size, :] = piece.astype(jnp.bfloat16)
+        o_ref[start:start + size, :] = jnp.where(low, heads[0], heads[1]).astype(jnp.bfloat16)
+        start += size
+
+def att_fwd(q, kv_own, kv_other, bias, blocks):
+    rows, width = q.shape
+    pairs = width // 128
+    heads = width // 64
+    return pl.pallas_call(
+        functools.partial(att_fwd_kernel, blocks),
+        grid=(pairs,),
+        in_specs=[
+            pl.BlockSpec((rows, 128), lambda i: (0, i)),
+            pl.BlockSpec((rows, 128), lambda i: (0, i)),
+            pl.BlockSpec((rows, 128), lambda i: (0, i)),
+            pl.BlockSpec((rows, 128), lambda i: (0, i + pairs)),
+            pl.BlockSpec((rows, 128), lambda i: (0, i + pairs)),
+            pl.BlockSpec((2 * rows, 128), lambda i: (0, 0)),
+        ],
+        out_specs=[
+            pl.BlockSpec((rows, 128), lambda i: (0, i)),
+            pl.BlockSpec((2, rows, 128), lambda i: (i, 0, 0)),
+        ],
+        out_shape=[
+            jax.ShapeDtypeStruct((rows, width), jnp.bfloat16),
+            jax.ShapeDtypeStruct((heads, rows, 128), jnp.bfloat16),
+        ],
+        scratch_shapes=[pltpu.VMEM((2 * rows, 256), jnp.bfloat16), pltpu.VMEM((2 * rows, 256), jnp.bfloat16)],
+        compiler_params=pltpu.CompilerParams(vmem_limit_bytes=56 * 2**20),
+        name="att_fwd",
+    )(q, kv_own, kv_other, kv_own, kv_other, bias)
+
+def att_bwd_kernel(blocks, q_ref, ko_ref, kp_ref, vo_ref, vp_ref, bias_ref, st_ref, do_ref, o_ref, dq_ref, dko_ref, dkp_ref, dvo_ref, dvp_ref, kbuf, vbuf, qx, dox, dkv):
+    rows = q_ref.shape[0]
+    kbuf[:rows, :128] = ko_ref[...]
+    kbuf[rows:, :128] = kp_ref[...]
+    vbuf[:rows, :128] = vo_ref[...]
+    vbuf[rows:, :128] = vp_ref[...]
+
+    @pl.when(pl.program_id(0) == 0)
+    def _():
+        kbuf[:, 128:] = bias_ref[...]
+        lane = lax.broadcasted_iota(jnp.int32, (2 * rows, 128), 1)
+        vbuf[:, 128:] = (lane < 3).astype(jnp.bfloat16)
+
+    lane = lax.broadcasted_iota(jnp.int32, (rows, 128), 1)
+    low = lane < 64
+    q = q_ref[...]
+    do = do_ref[...]
+    prod = do.astype(jnp.float32) * o_ref[...].astype(jnp.float32)
+    for h in range(2):
+        keep = low if h == 0 else jnp.logical_not(low)
+        qx[h, :, :128] = jnp.where(keep, q, jnp.zeros_like(q))
+        qx[h, :, 128:] = st_ref[h]
+        dox[h, :, :128] = jnp.where(keep, do, jnp.zeros_like(do))
+        total = -jnp.sum(jnp.where(keep, prod, 0.0), axis=-1, keepdims=True)
+        hi = total.astype(jnp.bfloat16).astype(jnp.float32)
+        mid = (total - hi).astype(jnp.bfloat16).astype(jnp.float32)
+        lo = total - hi - mid
+        piece = jnp.where(lane == 0, hi, jnp.where(lane == 1, mid, jnp.where(lane == 2, lo, 0.0)))
+        dox[h, :, 128:] = piece.astype(jnp.bfloat16)
+    start = 0
+    dqs = [None, None]
+    for size in blocks:
+        dk = None
+        dv = None
+        kb = kbuf[start:start + size, :]
+        vb = vbuf[start:start + size, :]
+        for h in range(2):
+            s = dotf(kb, qx[h], NT)
+            dp = dotf(vb, dox[h], NT)
+            p = jnp.exp(s)
+            ds = (p * dp).astype(jnp.bfloat16)
+            pl_ = p.astype(jnp.bfloat16)
+            dv_h = dotf(pl_, dox[h, :, :128], NN)
+            dk_h = dotf(ds, qx[h, :, :128], NN)
+            dv = dv_h if dv is None else dv + dv_h
+            dk = dk_h if dk is None else dk + dk_h
+            dq_h = dotf(kb[:, :128], ds, TN)
+            dqs[h] = dq_h if dqs[h] is None else dqs[h] + dq_h
+        dkv[0, start:start + size, :] = dk.astype(jnp.bfloat16)
+        dkv[1, start:start + size, :] = dv.astype(jnp.bfloat16)
+        start += size
+    dqs = [d.T for d in dqs]
+    dq_ref[...] = (jnp.where(low, dqs[0], dqs[1]) * 0.125).astype(jnp.bfloat16)
+    dko_ref[...] = dkv[0, :rows, :]
+    dkp_ref[...] = dkv[0, rows:, :]
+    dvo_ref[...] = dkv[1, :rows, :]
+    dvp_ref[...] = dkv[1, rows:, :]
+
+def att_bwd(q, kv_own, kv_other, bias, st, do, o, blocks):
+    rows, width = q.shape
+    pairs = width // 128
+    blk = pl.BlockSpec((rows, 128), lambda i: (0, i))
+    blk2 = pl.BlockSpec((rows, 128), lambda i: (0, i + pairs))
+    sd = jax.ShapeDtypeStruct((rows, width), jnp.bfloat16)
+    return pl.pallas_call(
+        functools.partial(att_bwd_kernel, blocks),
+        grid=(pairs,),
+        in_specs=[blk, blk, blk, blk2, blk2,
+            pl.BlockSpec((2 * rows, 128), lambda i: (0, 0)),
+            pl.BlockSpec((2, rows, 128), lambda i: (i, 0, 0)), blk, blk],
+        out_specs=[blk] * 5,
+        out_shape=[sd] * 5,
+        scratch_shapes=[pltpu.VMEM((2 * rows, 256), jnp.bfloat16), pltpu.VMEM((2 * rows, 256), jnp.bfloat16),
+            pltpu.VMEM((2, rows, 256), jnp.bfloat16), pltpu.VMEM((2, rows, 256), jnp.bfloat16), pltpu.VMEM((2, 2 * rows, 128), jnp.bfloat16)],
+        compiler_params=pltpu.CompilerParams(vmem_limit_bytes=56 * 2**20),
+        name="att_bwd",
+    )(q, kv_own, kv_other, kv_own, kv_other, bias, st, do, o)
+
+
+F32 = jnp.float32
+BF = jnp.bfloat16
+
+def norm_parts(v):
+    mean = jnp.mean(v, axis=-1, keepdims=True)
+    cen = v - mean
+    var = jnp.mean(cen * cen, axis=-1, keepdims=True)
+    r = lax.rsqrt(var + EPSILON)
+    return cen * r, r
+
+def norm_back(z, r, grad, gain):
+    e = grad * gain
+    return r * (e - jnp.mean(e, axis=-1, keepdims=True) - z * jnp.mean(e * z, axis=-1, keepdims=True))
+
+def mlp_kernel(att_ref, x_ref, cot_ref, live_ref, vec_ref, wp_ref, w1_ref, b1_ref, w2_ref,
+               mixed_ref, gmid_ref, gatt_ref, dwp_ref, dw1_ref, dw2_ref, small_ref, gb1_ref,
+               ao, n2, n2t, gm, acc, gn2):
+    step = pl.program_id(0)
+    last = pl.num_programs(0) - 1
+
+    @pl.when(step == 0)
+    def _():
+        a = dotf(att_ref[...], wp_ref[...], NN) + vec_ref[0:1, :]
+        ao[...] = a
+        mid = x_ref[...].astype(F32) + vec_ref[1:2, :] * a
+        gmid_ref[...] = mid
+        z, _r = norm_parts(mid)
+        n = (z * vec_ref[2:3, :] + vec_ref[3:4, :]).astype(BF)
+        n2[...] = n
+        n2t[...] = n.T
+        gm[...] = (cot_ref[...].astype(F32) * vec_ref[5:6, :]).astype(BF)
+        acc[...] = jnp.broadcast_to(vec_ref[4:5, :], acc.shape)
+        gn2[...] = jnp.zeros_like(gn2)
+
+    u = dotf(n2[...], w1_ref[...], NN) + b1_ref[...]
+    phi = 0.5 + 0.5 * lax.erf(u * 0.7071067811865476)
+    hid = (u * phi).astype(BF)
+    slope = phi + u * jnp.exp(u * u * -0.5) * 0.3989422804014327
+    gh = dotf(gm[...], w2_ref[...], NT)
+    gpf = gh * slope
+    gp = gpf.astype(BF)
+    gb1_ref[...] = jnp.sum(gp.astype(F32), axis=0, keepdims=True)
+    acc[...] += dotf(hid, w2_ref[...], NN)
+    gn2[...] += dotf(gp, w1_ref[...], NT)
+    dw2_ref[...] = dotf(hid, gm[...], TN).astype(BF)
+    dw1_ref[...] = dotf(n2t[...], gp, NN).astype(BF)
+
+    @pl.when(step == last)
+    def _():
+        out = acc[...]
+        cot = cot_ref[...].astype(F32)
+        live = live_ref[...]
+        x = x_ref[...].astype(F32)
+        mid = gmid_ref[...]
+        branch = vec_ref[5:6, :] * out
+        res = mid + branch
+        mixed_ref[...] = res.astype(BF)
+        col = lambda v: jnp.sum(v, axis=0, keepdims=True)
+        small_ref[0:1, :] = col(cot * out)
+        small_ref[1:2, :] = col(gm[...].astype(F32))
+        small_ref[8:9, :] = col(live * x * x)
+        ba = vec_ref[1:2, :] * ao[...]
+        small_ref[9:10, :] = col(live * ba * ba)
+        small_ref[10:11, :] = col(live * mid * mid)
+        small_ref[11:12, :] = col(live * branch * branch)
+        small_ref[12:13, :] = col(live * res * res)
+        z, r = norm_parts(mid)
+        g = gn2[...]
+        small_ref[2:3, :] = col(g * z)
+        small_ref[3:4, :] = col(g)
+        gmid = cot + norm_back(z, r, g, vec_ref[2:3, :])
+        gmid_ref[...] = gmid
+        small_ref[4:5, :] = col(gmid * ao[...])
+        gao = (gmid * vec_ref[1:2, :]).astype(BF)
+        small_ref[5:6, :] = col(gao.astype(F32))
+        gatt_ref[...] = dotf(gao, wp_ref[...], NT).astype(BF)
+        dwp_ref[...] = dotf(att_ref[...], gao, TN).astype(BF)
+
+def mlp(att, x, cot, live, vec, wp, w1, b1, w2, fc=512):
+    rows, width = att.shape
+    ff = w1.shape[1]
+    full = lambda s: pl.BlockSpec(s, lambda j: (0,) * len(s))
+    sd = jax.ShapeDtypeStruct
+    return pl.pallas_call(
+        mlp_kernel, grid=(ff // fc,),
+        in_specs=[full((rows, width)), full((rows, width)), full((rows, width)), full((rows, 1)), full((8, width)), full((width, width)),
+            pl.BlockSpec((width, fc), lambda j: (0, j)), pl.BlockSpec((1, fc), lambda j: (0, j)), pl.BlockSpec((fc, width), lambda j: (j, 0))],
+        out_specs=[full((rows, width)), full((rows, width)), full((rows, width)), full((width, width)),
+            pl.BlockSpec((width, fc), lambda j: (0, j)), pl.BlockSpec((fc, width), lambda j: (j, 0)), full((16, width)), pl.BlockSpec((1, fc), lambda j: (0, j))],
+        out_shape=[sd((rows, width), BF), sd((rows, width), F32), sd((rows, width), BF), sd((width, width), BF), sd((width, ff), BF), sd((ff, width), BF), sd((16, width), F32), sd((1, ff), F32)],
+        scratch_shapes=[pltpu.VMEM((rows, width), F32), pltpu.VMEM((rows, width), BF), pltpu.VMEM((width, rows), BF), pltpu.VMEM((rows, width), BF), pltpu.VMEM((rows, width), F32), pltpu.VMEM((rows, width), F32)],
+        compiler_params=pltpu.CompilerParams(vmem_limit_bytes=60 * 2**20), name="mlp",
+    )(att, x, cot, live, vec, wp, w1, b1, w2)
+
+def qkv_kernel(x_ref, vec_ref, w_ref, b_ref, n_ref, q_ref, kv_ref, n1):
+    step = pl.program_id(0)
+    @pl.when(step == 0)
+    def _():
+        z, _r = norm_parts(x_ref[...].astype(F32))
+        n = (z * vec_ref[0:1, :] + vec_ref[1:2, :]).astype(BF)
+        n1[...] = n
+        n_ref[...] = n
+    w = w_ref.shape[1]
+    y = (dotf(n1[...], w_ref[...], NN) + b_ref[...]).astype(BF)
+    @pl.when(step == 2)
+    def _():
+        q_ref[...] = y * jnp.asarray(0.125, BF)
+    @pl.when(step != 2)
+    def _():
+        kv_ref[...] = y
+
+def qkv(x, vec, w, b):
+    rows, width = x.shape
+    full = lambda s: pl.BlockSpec(s, lambda j: (0,) * len(s))
+    sd = jax.ShapeDtypeStruct
+    rot = lambda j: (0, (j + 1) % 3)
+    return pl.pallas_call(qkv_kernel, grid=(3,),
+        in_specs=[full((rows, width)), full((8, width)), pl.BlockSpec((width, width), rot), pl.BlockSpec((1, width), rot)],
+        out_specs=[full((rows, width)), full((rows, width)), pl.BlockSpec((rows, width), lambda j: (0, jnp.minimum(j, 1)))],
+        out_shape=[sd((rows, width), BF), sd((rows, width), BF), sd((rows, 2 * width), BF)],
+        scratch_shapes=[pltpu.VMEM((rows, width), BF)],
+        compiler_params=pltpu.CompilerParams(vmem_limit_bytes=56 * 2**20), name="qkv")(x, vec, w, b)
+
+def qback_kernel(dq_ref, dko_ref, dvo_ref, dkr_ref, dvr_ref, x_ref, n_ref, gmid_ref, vec_ref, w_ref, dw_ref, gx_ref, small_ref, nt, gn):
+    step = pl.program_id(0)
+    @pl.when(step == 0)
+    def _():
+        nt[...] = n_ref[...].T
+        gn[...] = jnp.zeros_like(gn)
+    def do(y):
+        dw_ref[...] = dotf(nt[...], y, NN).astype(BF)
+        gn[...] += dotf(y, w_ref[...], NT)
+        return jnp.sum(y.astype(F32), axis=0, keepdims=True)
+    @pl.when(step == 0)
+    def _():
+        small_ref[0:1, :] = do(dq_ref[...])
+    @pl.when(step == 1)
+    def _():
+        do((dko_ref[...].astype(F32) + dkr_ref[...].astype(F32)).astype(BF))
+    @pl.when(step == 2)
+    def _():
+        small_ref[1:2, :] = do((dvo_ref[...].astype(F32) + dvr_ref[...].astype(F32)).astype(BF))
+        z, r = norm_parts(x_ref[...].astype(F32))
+        g = gn[...]
+        small_ref[2:3, :] = jnp.sum(g * z, axis=0, keepdims=True)
+        small_ref[3:4, :] = jnp.sum(g, axis=0, keepdims=True)
+        gx_ref[...] = (gmid_ref[...] + norm_back(z, r, g, vec_ref[0:1, :])).astype(BF)
+
+def qback(dq, dko, dvo, dkr, dvr, x, n, gmid, vec, w):
+    rows, width = x.shape
+    full = lambda s: pl.BlockSpec(s, lambda j: (0,) * len(s))
+    sd = jax.ShapeDtypeStruct
+    f = full((rows, width))
+    return pl.pallas_call(qback_kernel, grid=(3,),
+        in_specs=[f] * 8 + [full((8, width)), pl.BlockSpec((width, width), lambda j: (0, j))],
+        out_specs=[pl.BlockSpec((width, width), lambda j: (0, j)), f, full((8, width))],
+        out_shape=[sd((width, 3 * width), BF), sd((rows, width), BF), sd((8, width), F32)],
+        scratch_shapes=[pltpu.VMEM((width, rows), BF), pltpu.VMEM((rows, width), F32)],
+        compiler_params=pltpu.CompilerParams(vmem_limit_bytes=60 * 2**20), name="qback")(dq, dko, dvo, dkr, dvr, x, n, gmid, vec, w)
+
+
+def relayout_pairs(groups, seq_count, turn):
+    half = seq_count // 2
+    pairs = []
+    for f in range(groups):
+        for z in range(seq_count):
+            image = (z + turn) % half
+            target = (f // 2 * 2 + z // half, f % 2 * half + image)
+            pairs.append((f * seq_count + z, target[0] * seq_count + target[1]))
+    return pairs
+
+
+AXES = ("fsdp", "seq")
+
+
+def fast_device(
+    tokens,
+    valid_len,
+    cotangent,
+    norm1_gain,
+    norm1_shift,
+    qkv_weight,
+    query_bias,
+    value_bias,
+    proj_weight,
+    proj_bias,
+    attn_scale,
+    norm2_gain,
+    norm2_shift,
+    fc1_weight,
+    fc1_bias,
+    fc2_weight,
+    fc2_bias,
+    mlp_scale,
+):
+    groups = lax.axis_size("fsdp")
+    seq_count = lax.axis_size("seq")
+    images_here, tok_here, width = tokens.shape
+    rows = 2 * tok_here
+    place = lax.axis_index("seq")
+    group = lax.axis_index("fsdp")
+    core = group % 2
+    turns = range(2)
+    pairs = [relayout_pairs(groups, seq_count, turn) for turn in turns]
+    back = [[(b, a) for a, b in pair] for pair in pairs]
+    swap = [(f, f ^ 1) for f in range(groups)]
+
+    def spread(block):
+        parts = []
+        for turn in turns:
+            sent = lax.dynamic_index_in_dim(block, (place + turn) % 2, 0, keepdims=False)
+            parts.append(lax.ppermute(sent, AXES, pairs[turn]))
+        return jnp.concatenate(parts, axis=0)
+
+    def collect(block):
+        got = [lax.ppermute(block[turn * tok_here : (turn + 1) * tok_here], AXES, back[turn]) for turn in turns]
+        even = place % 2 == 0
+        return jnp.stack([jnp.where(even, got[0], got[1]), jnp.where(even, got[1], got[0])])
+
+    small = jnp.concatenate(
+        [
+            norm1_gain, norm1_shift, query_bias, value_bias, proj_bias, attn_scale, norm2_gain, norm2_shift,
+            fc2_bias, mlp_scale, fc1_bias, (valid_len // 32).astype(BF), (valid_len % 32).astype(BF),
+        ]
+    )
+    x = spread(tokens)
+    small_all = lax.all_gather(small, "fsdp", axis=0).astype(F32)
+    part = width // groups
+    vectors = [small_all[:, i * part : (i + 1) * part].reshape(1, width) for i in range(10)]
+    gain1, shift1, bias_q, bias_v, bias_p, scale1, gain2, shift2, bias_2, scale2 = vectors
+    ff_part = fc1_bias.shape[0]
+    bias_1 = small_all[:, 10 * part : 10 * part + ff_part].reshape(1, -1)
+    rest = small_all[:, 10 * part + ff_part :].reshape(groups, 2, images_here)
+    lengths = (rest[:, 0] * 32 + rest[:, 1]).astype(jnp.int32)
+    column = group // 2
+    length = lax.dynamic_slice(lengths, (column * 2 + place // 2, place % 2), (1, 1))[0, 0]
+
+    def positions(which):
+        base = jnp.arange(tok_here, dtype=jnp.int32)
+        return jnp.concatenate([base + tok_here * (2 * which + (place + turn) % 2) for turn in turns])
+
+    own = positions(core)
+    keys_at = jnp.concatenate([own, positions(1 - core)])
+    lane = jnp.arange(128, dtype=jnp.int32)[None, :]
+    masked = jnp.where(keys_at < length, 0.0, -1e30)[:, None]
+    mask = jnp.where(lane == 0, masked, jnp.where(lane < 4, 1.0, 0.0)).astype(BF)
+    live = (own < length).astype(F32)[:, None]
+    zero = jnp.zeros((1, width), F32)
+    vec1 = jnp.concatenate([gain1, shift1] + [zero] * 6)
+    vec2 = jnp.concatenate([bias_p, scale1, gain2, shift2, bias_2, scale2, zero, zero])
+    bias_all = jnp.concatenate([bias_q, zero, bias_v], axis=1)
+
+    wq = lax.all_gather(qkv_weight, "fsdp", axis=0, tiled=True)
+    normed, q, kv = qkv(x, vec1, wq, bias_all)
+    kv_other = lax.ppermute(kv, "fsdp", swap)
+    cot = spread(cotangent)
+    wp = lax.all_gather(proj_weight, "fsdp", axis=0, tiled=True)
+    w1 = lax.all_gather(fc1_weight, "fsdp", axis=0, tiled=True)
+    w2 = lax.all_gather(fc2_weight, "fsdp", axis=0, tiled=True)
+    attended, stats = att_fwd(q, kv, kv_other, mask, FWD_BLOCKS(rows))
+    mixed, grad_mid, grad_att, dwp, dw1, dw2, small2, grad_b1 = mlp(attended, x, cot, live, vec2, wp, w1, bias_1, w2)
+    mixed_out = collect(mixed)
+    scatter = lambda v: lax.psum_scatter(v, "fsdp", scatter_dimension=0, tiled=True)
+    dw2_part = scatter(dw2)
+    dw1_part = scatter(dw1)
+    dwp_part = scatter(dwp)
+    dq, dko, dkp, dvo, dvp = att_bwd(q, kv, kv_other, mask, stats, grad_att, attended, (rows, rows))
+    dkr = lax.ppermute(dkp, "fsdp", swap)
+    dvr = lax.ppermute(dvp, "fsdp", swap)
+    dwq, grad_x, small1 = qback(dq, dko, dvo, dkr, dvr, x, normed, grad_mid, vec1, wq)
+    input_grad = collect(grad_x).astype(F32)
+    dwq_part = scatter(dwq)
+    totals = lax.psum((dw2_part, dw1_part, dwp_part), "seq")
+    total_q = lax.psum(dwq_part, "seq")
+    image = jnp.arange(groups * images_here, dtype=jnp.int32)
+    mine = image == (column * 2 + place // 2) * images_here + place % 2
+    squares = jnp.sum(small2[8:13], axis=1)
+    squares = jnp.where(mine[:, None], squares[None, :], 0.0)
+    sums = jnp.concatenate(
+        [
+            small1[2], small1[3], small1[0], small1[1], small2[5], small2[4], small2[2], small2[3],
+            small2[1], small2[0], grad_b1[0], squares.reshape(-1),
+        ]
+    )
+    sums = lax.psum(sums, AXES)
+    grads = [lax.dynamic_slice(sums, (i * width + group * part,), (part,)) for i in range(10)]
+    g_gain1, g_shift1, g_bq, g_bv, g_bp, g_scale1, g_gain2, g_shift2, g_b2, g_scale2 = grads
+    g_b1 = lax.dynamic_slice(sums, (10 * width + group * ff_part,), (ff_part,))
+    squares = sums[10 * width + groups * ff_part :].reshape(groups * images_here, 5)
+    squares = lax.dynamic_slice(squares, (group * images_here, 0), (images_here, 5))
+    rms = jnp.sqrt(squares / (valid_len.astype(F32)[:, None] * width))
+    return (
+        mixed_out, input_grad, rms, g_gain1, g_shift1, total_q.astype(F32), g_bq, g_bv, totals[2].astype(F32), g_bp,
+        g_scale1, g_gain2, g_shift2, totals[1].astype(F32), g_b1, totals[0].astype(F32), g_b2, g_scale2,
+    )
+
+
+def FWD_BLOCKS(rows):
+    first = (rows // 2 + 15) // 16 * 16
+    return (first, rows - first)
+
+
 def solution(mesh):
     in_specs = (
         P("fsdp", "seq", None),
@@ -380,6 +836,8 @@
         P("fsdp"),
         P("fsdp"),
     )
+    seq_count = mesh.shape["seq"]
+    paired = seq_count == 4 and mesh.shape["fsdp"] % 2 == 0
     return jax.shard_map(
-        per_device, mesh=mesh, in_specs=in_specs, out_specs=out_specs, check_vma=False
-    )
+        fast_device if paired else generic_device, mesh=mesh, in_specs=in_specs, out_specs=out_specs, check_vma=False
+    )

time: 1190 us -> 726 us (0.61)
  matrix products: 322 us -> 0 us
  Pallas kernels: 0 us -> 184 us
  blocking collectives: 230 us -> 129 us
  other arithmetic: 113 us -> 20.3 us
  local copies, waits for them, and re-layouts: 99.2 us -> 16.5 us
  waiting for transfers between devices: 387 us -> 341 us
    dot_general x40 -> x0, matrix products: 322 us -> none  [the longest x4 42 us: attend_back(): jnp.einsum('qhe,khe->hqk', part_q, keys_in, preferred_element_type=jnp.fl...]
    pallas_call x0 -> x5, Pallas kernels: none -> 184 us  [the longest x1 72.1 us: mlp(): pl.pallas_call(mlp_kernel, grid=(ff // fc,), in_specs=[full((rows, width)...]
    psum x1, waiting for transfers between devices: 167 us -> 40.2 us  [fast_device(): total_q = lax.psum(dwq_part, 'seq')]
    all_to_all x3 -> x0, waiting for transfers between devices: 116 us -> none  [the longest x1 94 us: per_device(): lax.all_to_all(projected.reshape(images_here, tok_here, 3, seq_count, hea...]
    reduce_scatter x4, waiting for transfers between devices: 92 us -> 205 us  [fast_device(): lax.psum_scatter(v, 'fsdp', scatter_dimension=0, tiled=True)]
    all_to_all x1 -> x0, blocking collectives: 97.8 us -> none  [per_device(): lax.all_to_all(for_sending(grad_qkv.reshape(images_here, length, 3, 1, he...]
    all_gather x11 -> x0, blocking collectives: 93.9 us -> none  [the longest x1 10.3 us: per_device(): lax.all_gather(norm1_gain, 'fsdp', axis=0, tiled=True)]
    psum x1, blocking collectives: 13.5 us -> 102 us  [fast_device(): sums = lax.psum(sums, AXES)]
  transfers between devices with their start and end apart: 12 -> 20, of which waited for: 5 -> 10; matrix products, arithmetic and copies ran while one was open for 40% -> 4% of each run, Pallas kernels for 0% -> 15%
where the time goes in v1:
time: 726 us; the launch traced here: 724 us
  waiting for transfers between devices  341 us (47%)
  Pallas kernels  184 us (25%)
  blocking collectives  129 us (18%)
  other arithmetic  20.3 us (3%)
  starting transfers between devices  18.5 us (3%)
  local copies, waits for them, and re-layouts  16.5 us (2%)
  between operations  15.3 us (2%)
    reduce_scatter x4, waiting for transfers between devices, fast_device(): lax.psum_scatter(v, 'fsdp', scatter_dimension=0, tiled=True)  205 us
    psum x1, blocking collectives, fast_device(): sums = lax.psum(sums, AXES)  102 us
    pallas_call x1, Pallas kernels, mlp(): pl.pallas_call(mlp_kernel, grid=(ff // fc,), in_specs=[full((rows, width)...  72.1 us
    all_gather x1, waiting for transfers between devices, fast_device(): w2 = lax.all_gather(fc2_weight, 'fsdp', axis=0, tiled=True)  56.2 us
    pallas_call x1, Pallas kernels, att_bwd(): pl.pallas_call(functools.partial(att_bwd_kernel, blocks), grid=(pairs,),...  50.8 us
    psum x1, waiting for transfers between devices, fast_device(): total_q = lax.psum(dwq_part, 'seq')  40.2 us
    pallas_call x1, Pallas kernels, att_fwd(): pl.pallas_call(functools.partial(att_fwd_kernel, blocks), grid=(pairs,),...  31.5 us
    unnamed x1, blocking collectives  27.4 us
  transfers between devices with their start and end apart: 20, of which 10 were waited for; matrix products, arithmetic and copies ran while one was open for 4% of the time, Pallas kernels for 15%

profile of v1, /device:TPU:0, one launch (start us, length us, event | category | flops | bytes accessed | tf_op | source)
XLA Modules:
  0.0 723.9 jit_solution(5041954633065617924)
XLA Ops:
  11.9 3.0 collective-permute-start.1
  16.6 27.4 %all-reduce = bf16[14368]{0:T(1024)(128)(2,1)S(1)} all-reduce(bf16[14368]{0:T(1024)(128)(2,1)S(1)} %dynamic-update-slice), channel_id=2, replica_groups=mesh['fsdp'=8,'seq'=4] {'fsdp'}, use_global_device_ids=true, to_apply=%add | all-reduce | flops 14368 | bytes 57472
  47.3 11.0 %all-gather.6.cloned.1.call-done.w_ref = bf16[1024,3072]{1,0:T(8,128)(2,1)} async-done(((bf16[128,3072]{1,0:T(8,128)(2,1)}), bf16[1024,3072]{1,0:T(8,128)(2,1)}) %all-gather.6.cloned.1.call-update) | async-done | bytes 6291472 | tf_op jit(solution)/shard_map/all_gather | solution.py:748
  58.4 10.9 %qkv.1 = (bf16[688,1024]{1,0:T(8,128)(2,1)}, bf16[688,1024]{1,0:T(8,128)(2,1)}, bf16[688,2048]{1,0:T(8,128)(2,1)}) custom-call(bf16[688,1024]{1,0:T(8,128)(2,1)} %copy-done.1, f32[8,1024]{1,0:T(8,128)} %maximum_maximum_fusion.vec_ref, bf16[1024,3072]{1,0:T(8,128)(2,1)} %all-gather.6.cloned.1.call-done.w_ref, f32[1,3072]{1,0:T(1,128)} %pad_maximum_fusion.2.b_ref), custom_call_target="tpu_custom_call" | custom-call | tf_op jit(solution)/shard_map/qkv/pallas_call | solution.py:612
  70.4 6.8 collective-permute-start.3
  83.0 1.6 copy.54.live_ref
  88.0 1.7 select_convert_fusion.bias_ref
  89.7 12.9 %collective-permute-done.4 = bf16[344,1024]{1,0:T(8,128)(2,1)} collective-permute-done((bf16[344,1024]{1,0:T(8,128)(2,1)S(1)}, bf16[344,1024]{1,0:T(8,128)(2,1)}, u32[]{:S(2)}, u32[]{:S(2)}) %collective-permute-start.4) | collective-permute-done | bytes 704544 | tf_op jit(solution)/shard_map/ppermute | solution.py:707
  102.6 2.5 pad_maximum_fusion.cot_ref
  106.6 31.5 %att_fwd.1 = (bf16[688,1024]{1,0:T(8,128)(2,1)}, bf16[16,688,128]{2,1,0:T(8,128)(2,1)}) custom-call(bf16[688,1024]{1,0:T(8,128)(2,1)} %get-tuple-element.39.q_ref, bf16[688,2048]{1,0:T(8,128)(2,1)} %get-tuple-element.40.ko_ref.vo_ref, bf16[688,2048]{1,0:T(8,128)(2,1)} %copy-done, bf16[688,2048]{1,0:T(8,128)(2,1)} %get-tuple-element.40.ko_ref.vo_ref, ...), custom_call_target="tpu_custom_call" | custom-call | tf_op jit(solution)/shard_map/att_fwd/pallas_call | solution.py:393
  138.1 6.3 all-gather.10.cloned.1.call-done.w1_ref
  144.4 56.2 %all-gather.12.cloned.1.call-done.w2_ref = bf16[4096,1024]{1,0:T(8,128)(2,1)} async-done(((bf16[512,1024]{1,0:T(8,128)(2,1)}), bf16[4096,1024]{1,0:T(8,128)(2,1)}) %all-gather.12.cloned.1.call-update) | async-done | bytes 8388624 | tf_op jit(solution)/shard_map/all_gather | solution.py:754
  200.6 72.1 %mlp.1 = (bf16[688,1024]{1,0:T(8,128)(2,1)}, f32[688,1024]{1,0:T(8,128)}, bf16[688,1024]{1,0:T(8,128)(2,1)}, bf16[1024,1024]{1,0:T(8,128)(2,1)}, bf16[1024,4096]...) custom-call(bf16[688,1024]{1,0:T(8,128)(2,1)} %get-tuple-element.41.att_ref.o_ref, ...), custom_call_target="tpu_custom_call" | custom-call | tf_op jit(solution)/shard_map/mlp/pallas_call | solution.py:579
  272.8 50.8 %att_bwd.1 = (bf16[688,1024]{1,0:T(8,128)(2,1)}, bf16[688,1024]{1,0:T(8,128)(2,1)}, bf16[688,1024]{1,0:T(8,128)(2,1)}, bf16[688,1024]{1,0:T(8,128)(2,1)}, bf16[688,1024]{1,0:T(8,128)(2,1)}) custom-call(bf16[688,1024]{1,0:T(8,128)(2,1)} %get-tuple-element.39.q_ref, bf16[688,2048]{1,0:T(8,128)(2,1)} %get-tuple-element.40.ko_ref.vo_ref, ...), custom_call_target="tpu_custom_call" | custom-call | tf_op jit(solution)/shard_map/att_bwd/pallas_call | solution.py:481
  324.2 2.9 collective-permute-done.7.dkr_ref
  327.1 2.0 collective-permute-done.8.dvr_ref
  330.2 18.4 %qback.1 = (bf16[1024,3072]{1,0:T(8,128)(2,1)}, bf16[688,1024]{1,0:T(8,128)(2,1)}, f32[8,1024]{1,0:T(8,128)}) custom-call(bf16[688,1024]{1,0:T(8,128)(2,1)} %get-tuple-element.45.dq_ref, bf16[688,1024]{1,0:T(8,128)(2,1)} %get-tuple-element.46.dko_ref, bf16[688,1024]{1,0:T(8,128)(2,1)} %get-tuple-element.47.dvo_ref, bf16[688,1024]{1,0:T(8,128)(2,1)} %copy-done.6, ...), custom_call_target="tpu_custom_call" | custom-call | tf_op jit(solution)/shard_map/qback/pallas_call | solution.py:649
  355.1 55.3 %reduce-scatter.5.cloned.1.call-done = bf16[128,3072]{1,0:T(8,128)(2,1)} async-done(((bf16[1024,3072]{1,0:T(8,128)(2,1)}), bf16[128,3072]{1,0:T(8,128)(2,1)}) %reduce-scatter.5.cloned.1.call-update) | async-done | bytes 786448 | tf_op jit(solution)/shard_map/reduce_scatter | solution.py:758
  410.4 74.8 %reduce-scatter.11.cloned.1.call-done = bf16[512,1024]{1,0:T(8,128)(2,1)} async-done(((bf16[4096,1024]{1,0:T(8,128)(2,1)}), bf16[512,1024]{1,0:T(8,128)(2,1)}) %reduce-scatter.11.cloned.1.call-update) | async-done | bytes 1048592 | tf_op jit(solution)/shard_map/reduce_scatter | solution.py:758
  485.2 75.1 %reduce-scatter.9.cloned.1.call-done = bf16[128,4096]{1,0:T(8,128)(2,1)} async-done(((bf16[1024,4096]{1,0:T(8,128)(2,1)}), bf16[128,4096]{1,0:T(8,128)(2,1)}) %reduce-scatter.9.cloned.1.call-update) | async-done | bytes 1048592 | tf_op jit(solution)/shard_map/reduce_scatter | solution.py:758
  565.1 101.5 %psum.35 = f32[14416]{0:T(1024)S(1)} all-reduce(f32[14416]{0:T(1024)S(1)} %constant_dynamic-update-slice_fusion.3), channel_id=1, replica_groups=mesh['fsdp'=8,'seq'=4] {'fsdp','seq'}, use_global_device_ids=true, to_apply=%region_1.2 | all-reduce | flops 14416 | bytes 115328 | tf_op jit(solution)/shard_map/psum | solution.py:780
  668.8 1.7 maximum_convert_fusion
  670.5 40.2 %all-reduce.4.cloned.1.call-done = (bf16[128,3072]{1,0:T(8,128)(2,1)}, bf16[128,1024]{1,0:T(8,128)(2,1)}, bf16[128,4096]{1,0:T(8,128)(2,1)}, bf16[512,1024]{1,0:T(8,128)(2,1)}) async-done(((bf16[128,3072]{1,0:T(8,128)(2,1)}, bf16[128,1024]{1,0:T(8,128)(2,1)}, bf16[128,4096]{1,0:T(8,128)(2,1)}, bf16[512,1024]{1,0:T(8,128)(2,1)}), (bf16[128,3072]{1,0:T(8,128)(2,1)}, bf16[128,1024]{1,0:T(8,128)(2,1)}, ...) | async-done | bytes 3145744 | tf_op jit(solution)/shard_map/psum | solution.py:769
  710.7 2.8 convert_element_type.54
  (160 shorter events, 39.2 us)
Async XLA Ops:
  7.2 51.2 %all-gather.6.cloned.1.call-start = ((), (), s32[]{:S(2)}) async-start(), calls=%async_computation.4 | async-start | bytes 7077888 | tf_op jit(solution)/shard_map/all_gather | solution.py:748
  7.9 130.2 %all-gather.8.cloned.1.call-start = ((), (), s32[]{:S(2)}) async-start(), calls=%async_computation.5 | async-start | bytes 2359296 | tf_op jit(solution)/shard_map/all_gather | solution.py:752
  8.7 135.8 %all-gather.10.cloned.1.call-start = ((), (), s32[]{:S(2)}) async-start(), calls=%async_computation.6 | async-start | bytes 9437184 | tf_op jit(solution)/shard_map/all_gather | solution.py:753
  9.4 191.2 %all-gather.12.cloned.1.call-start = ((), (), s32[]{:S(2)}) async-start(), calls=%async_computation.7 | async-start | bytes 9437184 | tf_op jit(solution)/shard_map/all_gather | solution.py:754
  10.0 345.1 %reduce-scatter.7.cloned.1.call-start = ((), (), s32[]{:S(2)}) async-start(), calls=%async_computation.9 | async-start | bytes 2359296 | tf_op jit(solution)/shard_map/reduce_scatter | solution.py:758
  10.1 6.0 copy-start.14
  10.3 35.7 %collective-permute-start = (bf16[344,1024]{1,0:T(8,128)(2,1)S(1)}, bf16[344,1024]{1,0:T(8,128)(2,1)}, u32[]{:S(2)}, u32[]{:S(2)}) collective-permute-start(bf16[344,1024]{1,0:T(8,128)(2,1)S(1)} %get-tuple-element.75), channel_id=1, source_target_pairs={{0,0},{1,1},{2,4},{3,5},{4,2},{5,3},{6,6},{7,7},{8,8},{9,9},{10,12... | collective-permute-start | bytes 2113544 | tf_op jit(solution)/shard_map/ppermute | solution.py:707
  11.9 35.4 %collective-permute-start.1 = (bf16[344,1024]{1,0:T(8,128)(2,1)S(1)}, bf16[344,1024]{1,0:T(8,128)(2,1)S(1)}, u32[]{:S(2)}, u32[]{:S(2)}) collective-permute-start(bf16[344,1024]{1,0:T(8,128)(2,1)S(1)} %get-tuple-element.74), channel_id=1, source_target_pairs={{0,1},{1,0},{2,5},{3,4},{4,3},{5,2},{6,7},{7,6},{8,9},{9,8},{10,13... | collective-permute-start | bytes 2113544 | tf_op jit(solution)/shard_map/ppermute | solution.py:707
  47.3 11.0 %copy-start.1 = (bf16[688,1024]{1,0:T(8,128)(2,1)}, bf16[688,1024]{1,0:T(8,128)(2,1)S(1)}, u32[]{:S(2)}) copy-start(bf16[688,1024]{1,0:T(8,128)(2,1)S(1)} %constant_dynamic-update-slice_fusion.x_ref) | copy-start | bytes 4227076
  58.4 11.1 %copy-start.3 = (bf16[2,344,1024]{2,1,0:T(8,128)(2,1)S(1)}, bf16[2,344,1024]{2,1,0:T(8,128)(2,1)}, u32[]{:S(2)}) copy-start(bf16[2,344,1024]{2,1,0:T(8,128)(2,1)} %param.20) | copy-start | bytes 4227076
  69.2 9.4 %slice-start = ((f32[8,1796]{1,0:T(8,128)}), f32[8,4]{1,0:T(8,128)S(1)}, s32[]{:S(2)}) async-start(f32[8,1796]{1,0:T(8,128)} %copy-done.11), calls=%async_computation.13 | async-start | bytes 8192 | tf_op jit(solution)/shard_map/slice | solution.py:728
  69.2 35.8 %collective-permute-start.2 = (bf16[688,2048]{1,0:T(8,128)(2,1)}, bf16[688,2048]{1,0:T(8,128)(2,1)S(1)}, u32[]{:S(2)}, u32[]{:S(2)}) collective-permute-start(bf16[688,2048]{1,0:T(8,128)(2,1)} %get-tuple-element.40.ko_ref.vo_ref), channel_id=1, source_target_pairs={{0,4},{4,0},{8,12},{12,8},{16,20},{20,16},{24,28},{28,24},{1,5},{5... | collective-permute-start | bytes 8454152 | tf_op jit(solution)/shard_map/ppermute | solution.py:750
  70.4 19.2 %collective-permute-start.3 = (bf16[344,1024]{1,0:T(8,128)(2,1)}, bf16[344,1024]{1,0:T(8,128)(2,1)}, u32[]{:S(2)}, u32[]{:S(2)}) collective-permute-start(bf16[344,1024]{1,0:T(8,128)(2,1)} %get-tuple-element.72), channel_id=1, source_target_pairs={{0,0},{1,1},{2,4},{3,5},{4,2},{5,3},{6,6},{7,7},{8,8},{9,9},{10,12... | collective-permute-start | bytes 2113544 | tf_op jit(solution)/shard_map/ppermute | solution.py:707
  77.2 25.3 %collective-permute-start.4 = (bf16[344,1024]{1,0:T(8,128)(2,1)S(1)}, bf16[344,1024]{1,0:T(8,128)(2,1)}, u32[]{:S(2)}, u32[]{:S(2)}) collective-permute-start(bf16[344,1024]{1,0:T(8,128)(2,1)S(1)} %get-tuple-element.73), channel_id=1, source_target_pairs={{0,1},{1,0},{2,5},{3,4},{4,3},{5,2},{6,7},{7,6},{8,9},{9,8},{10,13... | collective-permute-start | bytes 2113544 | tf_op jit(solution)/shard_map/ppermute | solution.py:707
  272.7 137.7 %reduce-scatter.5.cloned.1.call-start = ((), (), s32[]{:S(2)}) async-start(), calls=%async_computation.8 | async-start | bytes 7077888 | tf_op jit(solution)/shard_map/reduce_scatter | solution.py:758
  323.6 3.5 collective-permute-start.7
  323.9 5.1 collective-permute-start.8
  348.6 136.7 %reduce-scatter.11.cloned.1.call-start = ((), (), s32[]{:S(2)}) async-start(), calls=%async_computation.11 | async-start | bytes 9437184 | tf_op jit(solution)/shard_map/reduce_scatter | solution.py:758
  349.3 211.1 %reduce-scatter.9.cloned.1.call-start = ((), (), s32[]{:S(2)}) async-start(), calls=%async_computation.10 | async-start | bytes 9437184 | tf_op jit(solution)/shard_map/reduce_scatter | solution.py:758
  350.1 360.6 %all-reduce.4.cloned.1.call-start = ((), (), s32[]{:S(2)}) async-start(), calls=%async_computation.12 | async-start | bytes 6291456 | tf_op jit(solution)/shard_map/psum | solution.py:769
  350.8 209.7 %collective-permute-start.5 = (bf16[344,1024]{1,0:T(8,128)(2,1)S(1)}, bf16[344,1024]{1,0:T(8,128)(2,1)S(1)}, u32[]{:S(2)}, u32[]{:S(2)}) collective-permute-start(bf16[344,1024]{1,0:T(8,128)(2,1)S(1)} %get-tuple-element.70), channel_id=1, source_target_pairs={{0,0},{1,1},{4,2},{5,3},{2,4},{3,5},{6,6},{7,7},{8,8},{9,9},{12,10... | collective-permute-start | bytes 2113544 | tf_op jit(solution)/shard_map/ppermute | solution.py:711
  351.5 209.0 %collective-permute-start.6 = (bf16[344,1024]{1,0:T(8,128)(2,1)S(1)}, bf16[344,1024]{1,0:T(8,128)(2,1)S(1)}, u32[]{:S(2)}, u32[]{:S(2)}) collective-permute-start(bf16[344,1024]{1,0:T(8,128)(2,1)S(1)} %get-tuple-element.71), channel_id=1, source_target_pairs={{1,0},{0,1},{5,2},{4,3},{3,4},{2,5},{7,6},{6,7},{9,8},{8,9},{13,10... | collective-permute-start | bytes 2113544 | tf_op jit(solution)/shard_map/ppermute | solution.py:711
  562.7 106.0 %collective-permute-start.10 = (bf16[344,1024]{1,0:T(8,128)(2,1)S(1)}, bf16[344,1024]{1,0:T(8,128)(2,1)S(1)}, u32[]{:S(2)}, u32[]{:S(2)}) collective-permute-start(bf16[344,1024]{1,0:T(8,128)(2,1)S(1)} %get-tuple-element.67), channel_id=1, source_target_pairs={{1,0},{0,1},{5,2},{4,3},{3,4},{2,5},{7,6},{6,7},{9,8},{8,9},{13,10... | collective-permute-start | bytes 2113544 | tf_op jit(solution)/shard_map/ppermute | solution.py:711
  564.2 104.5 %collective-permute-start.9 = (bf16[344,1024]{1,0:T(8,128)(2,1)S(1)}, bf16[344,1024]{1,0:T(8,128)(2,1)S(1)}, u32[]{:S(2)}, u32[]{:S(2)}) collective-permute-start(bf16[344,1024]{1,0:T(8,128)(2,1)S(1)} %get-tuple-element.66), channel_id=1, source_target_pairs={{0,0},{1,1},{4,2},{5,3},{2,4},{3,5},{6,6},{7,7},{8,8},{9,9},{12,10... | collective-permute-start | bytes 2113544 | tf_op jit(solution)/shard_map/ppermute | solution.py:711
  (25 other events, 98.2 us)
Sparse Core Ops, SparseCore 0:
  9.9 48.3 all-gather.5
  60.2 27.8 all-gather.7
  90.0 54.3 all-gather.9
  146.2 54.3 all-gather.11
  272.9 41.2 reduce-scatter.6
  348.7 61.7 reduce-scatter.4
  413.9 71.2 reduce-scatter.10
  489.1 71.2 reduce-scatter.8
  563.0 147.6 all-reduce.3

commit v2 on v1

--- a/solution.py
+++ b/solution.py
@@ -414,85 +414,6 @@
         name="att_fwd",
     )(q, kv_own, kv_other, kv_own, kv_other, bias)
 
-def att_bwd_kernel(blocks, q_ref, ko_ref, kp_ref, vo_ref, vp_ref, bias_ref, st_ref, do_ref, o_ref, dq_ref, dko_ref, dkp_ref, dvo_ref, dvp_ref, kbuf, vbuf, qx, dox, dkv):
-    rows = q_ref.shape[0]
-    kbuf[:rows, :128] = ko_ref[...]
-    kbuf[rows:, :128] = kp_ref[...]
-    vbuf[:rows, :128] = vo_ref[...]
-    vbuf[rows:, :128] = vp_ref[...]
-
-    @pl.when(pl.program_id(0) == 0)
-    def _():
-        kbuf[:, 128:] = bias_ref[...]
-        lane = lax.broadcasted_iota(jnp.int32, (2 * rows, 128), 1)
-        vbuf[:, 128:] = (lane < 3).astype(jnp.bfloat16)
-
-    lane = lax.broadcasted_iota(jnp.int32, (rows, 128), 1)
-    low = lane < 64
-    q = q_ref[...]
-    do = do_ref[...]
-    prod = do.astype(jnp.float32) * o_ref[...].astype(jnp.float32)
-    for h in range(2):
-        keep = low if h == 0 else jnp.logical_not(low)
-        qx[h, :, :128] = jnp.where(keep, q, jnp.zeros_like(q))
-        qx[h, :, 128:] = st_ref[h]
-        dox[h, :, :128] = jnp.where(keep, do, jnp.zeros_like(do))
-        total = -jnp.sum(jnp.where(keep, prod, 0.0), axis=-1, keepdims=True)
-        hi = total.astype(jnp.bfloat16).astype(jnp.float32)
-        mid = (total - hi).astype(jnp.bfloat16).astype(jnp.float32)
-        lo = total - hi - mid
-        piece = jnp.where(lane == 0, hi, jnp.where(lane == 1, mid, jnp.where(lane == 2, lo, 0.0)))
-        dox[h, :, 128:] = piece.astype(jnp.bfloat16)
-    start = 0
-    dqs = [None, None]
-    for size in blocks:
-        dk = None
-        dv = None
-        kb = kbuf[start:start + size, :]
-        vb = vbuf[start:start + size, :]
-        for h in range(2):
-            s = dotf(kb, qx[h], NT)
-            dp = dotf(vb, dox[h], NT)
-            p = jnp.exp(s)
-            ds = (p * dp).astype(jnp.bfloat16)
-            pl_ = p.astype(jnp.bfloat16)
-            dv_h = dotf(pl_, dox[h, :, :128], NN)
-            dk_h = dotf(ds, qx[h, :, :128], NN)
-            dv = dv_h if dv is None else dv + dv_h
-            dk = dk_h if dk is None else dk + dk_h
-            dq_h = dotf(kb[:, :128], ds, TN)
-            dqs[h] = dq_h if dqs[h] is None else dqs[h] + dq_h
-        dkv[0, start:start + size, :] = dk.astype(jnp.bfloat16)
-        dkv[1, start:start + size, :] = dv.astype(jnp.bfloat16)
-        start += size
-    dqs = [d.T for d in dqs]
-    dq_ref[...] = (jnp.where(low, dqs[0], dqs[1]) * 0.125).astype(jnp.bfloat16)
-    dko_ref[...] = dkv[0, :rows, :]
-    dkp_ref[...] = dkv[0, rows:, :]
-    dvo_ref[...] = dkv[1, :rows, :]
-    dvp_ref[...] = dkv[1, rows:, :]
-
-def att_bwd(q, kv_own, kv_other, bias, st, do, o, blocks):
-    rows, width = q.shape
-    pairs = width // 128
-    blk = pl.BlockSpec((rows, 128), lambda i: (0, i))
-    blk2 = pl.BlockSpec((rows, 128), lambda i: (0, i + pairs))
-    sd = jax.ShapeDtypeStruct((rows, width), jnp.bfloat16)
-    return pl.pallas_call(
-        functools.partial(att_bwd_kernel, blocks),
-        grid=(pairs,),
-        in_specs=[blk, blk, blk, blk2, blk2,
-            pl.BlockSpec((2 * rows, 128), lambda i: (0, 0)),
-            pl.BlockSpec((2, rows, 128), lambda i: (i, 0, 0)), blk, blk],
-        out_specs=[blk] * 5,
-        out_shape=[sd] * 5,
-        scratch_shapes=[pltpu.VMEM((2 * rows, 256), jnp.bfloat16), pltpu.VMEM((2 * rows, 256), jnp.bfloat16),
-            pltpu.VMEM((2, rows, 256), jnp.bfloat16), pltpu.VMEM((2, rows, 256), jnp.bfloat16), pltpu.VMEM((2, 2 * rows, 128), jnp.bfloat16)],
-        compiler_params=pltpu.CompilerParams(vmem_limit_bytes=56 * 2**20),
-        name="att_bwd",
-    )(q, kv_own, kv_other, kv_own, kv_other, bias, st, do, o)
-
-
 F32 = jnp.float32
 BF = jnp.bfloat16
 
@@ -508,9 +429,11 @@
     return r * (e - jnp.mean(e, axis=-1, keepdims=True) - z * jnp.mean(e * z, axis=-1, keepdims=True))
 
 def mlp_kernel(att_ref, x_ref, cot_ref, live_ref, vec_ref, wp_ref, w1_ref, b1_ref, w2_ref,
-               mixed_ref, gmid_ref, gatt_ref, dwp_ref, dw1_ref, dw2_ref, small_ref, gb1_ref,
+               mixed_ref, gmid_ref, gatt_ref, dwp_ref, dw1_ref, dw2_ref, small_ref,
                ao, n2, n2t, gm, acc, gn2):
     step = pl.program_id(0)
+    part = att_ref.shape[1] // small_ref.shape[0]
+    half = att_ref.shape[0] // 2
     last = pl.num_programs(0) - 1
 
     @pl.when(step == 0)
@@ -534,7 +457,9 @@
     gh = dotf(gm[...], w2_ref[...], NT)
     gpf = gh * slope
     gp = gpf.astype(BF)
-    gb1_ref[...] = jnp.sum(gp.astype(F32), axis=0, keepdims=True)
+    gb1 = jnp.sum(gp.astype(F32), axis=0, keepdims=True)
+    for i in range(gb1.shape[1] // part):
+        small_ref[step, 10 + i:11 + i, :] = gb1[:, i * part:(i + 1) * part]
     acc[...] += dotf(hid, w2_ref[...], NN)
     gn2[...] += dotf(gp, w1_ref[...], NT)
     dw2_ref[...] = dotf(hid, gm[...], TN).astype(BF)
@@ -549,52 +474,67 @@
         mid = gmid_ref[...]
         branch = vec_ref[5:6, :] * out
         res = mid + branch
-        mixed_ref[...] = res.astype(BF)
+        low = res.astype(BF)
+        mixed_ref[0, :half] = low[:half]
+        mixed_ref[1, :half] = low[half:]
+        mixed_ref[:, half:] = jnp.zeros_like(mixed_ref[:, half:])
+        groups = small_ref.shape[0]
+
+        def put(row, v):
+            for i in range(groups):
+                small_ref[i, row:row + 1, :] = v[:, i * part:(i + 1) * part]
+
         col = lambda v: jnp.sum(v, axis=0, keepdims=True)
-        small_ref[0:1, :] = col(cot * out)
-        small_ref[1:2, :] = col(gm[...].astype(F32))
-        small_ref[8:9, :] = col(live * x * x)
+        put(0, col(cot * out))
+        put(1, col(gm[...].astype(F32)))
         ba = vec_ref[1:2, :] * ao[...]
-        small_ref[9:10, :] = col(live * ba * ba)
-        small_ref[10:11, :] = col(live * mid * mid)
-        small_ref[11:12, :] = col(live * branch * branch)
-        small_ref[12:13, :] = col(live * res * res)
+        place = lax.axis_index("seq")
+        owner = lax.axis_index("fsdp") // 2 * 2 + place // 2
+        lane = lax.broadcasted_iota(jnp.int32, (1, part), 1)
+        line = jnp.zeros((1, part), F32)
+        for i, v in enumerate((x, ba, mid, branch, res)):
+            line = jnp.where(lane == place % 2 * 5 + i, jnp.sum(col(live * v * v), axis=1, keepdims=True), line)
+        for i in range(groups):
+            small_ref[i, 14:15, :] = jnp.where(owner == i, line, 0.0)
+            small_ref[i, 15:16, :] = jnp.zeros_like(line)
         z, r = norm_parts(mid)
         g = gn2[...]
-        small_ref[2:3, :] = col(g * z)
-        small_ref[3:4, :] = col(g)
+        put(2, col(g * z))
+        put(3, col(g))
         gmid = cot + norm_back(z, r, g, vec_ref[2:3, :])
         gmid_ref[...] = gmid
-        small_ref[4:5, :] = col(gmid * ao[...])
+        put(4, col(gmid * ao[...]))
         gao = (gmid * vec_ref[1:2, :]).astype(BF)
-        small_ref[5:6, :] = col(gao.astype(F32))
+        put(5, col(gao.astype(F32)))
         gatt_ref[...] = dotf(gao, wp_ref[...], NT).astype(BF)
         dwp_ref[...] = dotf(att_ref[...], gao, TN).astype(BF)
 
-def mlp(att, x, cot, live, vec, wp, w1, b1, w2, fc=512):
+def mlp(att, x, cot, live, vec, wp, w1, b1, w2, groups):
     rows, width = att.shape
     ff = w1.shape[1]
+    fc = ff // groups
+    pad = (rows // 2 + 15) // 16 * 16
     full = lambda s: pl.BlockSpec(s, lambda j: (0,) * len(s))
     sd = jax.ShapeDtypeStruct
     return pl.pallas_call(
         mlp_kernel, grid=(ff // fc,),
         in_specs=[full((rows, width)), full((rows, width)), full((rows, width)), full((rows, 1)), full((8, width)), full((width, width)),
             pl.BlockSpec((width, fc), lambda j: (0, j)), pl.BlockSpec((1, fc), lambda j: (0, j)), pl.BlockSpec((fc, width), lambda j: (j, 0))],
-        out_specs=[full((rows, width)), full((rows, width)), full((rows, width)), full((width, width)),
-            pl.BlockSpec((width, fc), lambda j: (0, j)), pl.BlockSpec((fc, width), lambda j: (j, 0)), full((16, width)), pl.BlockSpec((1, fc), lambda j: (0, j))],
-        out_shape=[sd((rows, width), BF), sd((rows, width), F32), sd((rows, width), BF), sd((width, width), BF), sd((width, ff), BF), sd((ff, width), BF), sd((16, width), F32), sd((1, ff), F32)],
+        out_specs=[full((2, pad, width)), full((rows, width)), full((rows, width)), full((width, width)),
+            pl.BlockSpec((width, fc), lambda j: (0, j)), pl.BlockSpec((fc, width), lambda j: (j, 0)), full((groups, 16, width // groups))],
+        out_shape=[sd((2, pad, width), BF), sd((rows, width), F32), sd((rows, width), BF), sd((width, width), BF), sd((width, ff), BF), sd((ff, width), BF), sd((groups, 16, width // groups), F32)],
         scratch_shapes=[pltpu.VMEM((rows, width), F32), pltpu.VMEM((rows, width), BF), pltpu.VMEM((width, rows), BF), pltpu.VMEM((rows, width), BF), pltpu.VMEM((rows, width), F32), pltpu.VMEM((rows, width), F32)],
         compiler_params=pltpu.CompilerParams(vmem_limit_bytes=60 * 2**20), name="mlp",
     )(att, x, cot, live, vec, wp, w1, b1, w2)
 
-def qkv_kernel(x_ref, vec_ref, w_ref, b_ref, n_ref, q_ref, kv_ref, n1):
+def qkv_kernel(x_ref, vec_ref, w_ref, b_ref, nt_ref, q_ref, kv_ref, n1):
     step = pl.program_id(0)
     @pl.when(step == 0)
     def _():
         z, _r = norm_parts(x_ref[...].astype(F32))
         n = (z * vec_ref[0:1, :] + vec_ref[1:2, :]).astype(BF)
         n1[...] = n
-        n_ref[...] = n
+        nt_ref[...] = n.T
     w = w_ref.shape[1]
     y = (dotf(n1[...], w_ref[...], NN) + b_ref[...]).astype(BF)
     @pl.when(step == 2)
@@ -611,47 +551,480 @@
     rot = lambda j: (0, (j + 1) % 3)
     return pl.pallas_call(qkv_kernel, grid=(3,),
         in_specs=[full((rows, width)), full((8, width)), pl.BlockSpec((width, width), rot), pl.BlockSpec((1, width), rot)],
-        out_specs=[full((rows, width)), full((rows, width)), pl.BlockSpec((rows, width), lambda j: (0, jnp.minimum(j, 1)))],
-        out_shape=[sd((rows, width), BF), sd((rows, width), BF), sd((rows, 2 * width), BF)],
+        out_specs=[full((width, rows)), full((rows, width)), pl.BlockSpec((rows, width), lambda j: (0, jnp.minimum(j, 1)))],
+        out_shape=[sd((width, rows), BF), sd((rows, width), BF), sd((rows, 2 * width), BF)],
         scratch_shapes=[pltpu.VMEM((rows, width), BF)],
         compiler_params=pltpu.CompilerParams(vmem_limit_bytes=56 * 2**20), name="qkv")(x, vec, w, b)
 
-def qback_kernel(dq_ref, dko_ref, dvo_ref, dkr_ref, dvr_ref, x_ref, n_ref, gmid_ref, vec_ref, w_ref, dw_ref, gx_ref, small_ref, nt, gn):
+
+MESH = pl.DeviceIdType.MESH
+
+
+def places():
+    f = lax.axis_index("fsdp")
+    z = lax.axis_index("seq")
+    core = f % 2
+    dx = 2 - 4 * (f // 2 % 2)
+    dy = 4 - 8 * (f // 4)
+    da = (1 - core) * dx + core * dy
+    db = core * dx + (1 - core) * dy
+    mate = f + 1 - 2 * core
+    return f, z, mate, da, db
+
+
+def reduce_scratch(rows, cols, chunks, kind, copied=True):
+    dma = pltpu.SemaphoreType.DMA
+    bufs = [pltpu.VMEM((n, rows, cols), kind) for n in (4, 3, 2)] + [pltpu.VMEM((rows, cols), kind)]
+    sems = [dma((chunks, n)) for n in (4, 4, 3, 3, 2, 2)]
+    if copied:
+        bufs.append(pltpu.VMEM((4, rows, cols), kind))
+        sems.append(dma((chunks, 4)))
+    return bufs + sems
+
+
+REDUCE_REFS = 10
+REDUCE_REFS_COPIED = 12
+
+
+def reduce_steps(src, out, scratch, cuts, copied=True):
+    if copied:
+        yours, came, zin, tot, mine, ex_send, ex_recv, l_send, l_recv, z_send, z_recv, load_sem = scratch
+    else:
+        yours, came, zin, tot, ex_send, ex_recv, l_send, l_recv, z_send, z_recv = scratch
+    f, z, mate, da, db = places()
+    own = (f + da + db, f + db, f + da, f)
+    other = (mate + da + db, mate + da, mate + db, mate)
+    outer = z % 3 == 0
+    inner = z % 3 != 0
+
+    def remote(a, b, s, r, dev):
+        return pltpu.make_async_remote_copy(src_ref=a, dst_ref=b, send_sem=s, recv_sem=r, device_id=dev, device_id_type=MESH)
+
+    def steps(k, lo, size):
+        at = pl.ds(lo, size)
+
+        def held(m):
+            return mine.at[m, at] if copied else src.at[own[m], at]
+
+        def load(m):
+            return pltpu.make_async_copy(src.at[own[m], at], mine.at[m, at], load_sem.at[k, m])
+
+        def swap(m):
+            return remote(src.at[other[m], at], yours.at[m, at], ex_send.at[k, m], ex_recv.at[k, m], (mate, z))
+
+        def hop(i):
+            return remote(held(i), came.at[i, at], l_send.at[k, i], l_recv.at[k, i], (f + (da if i == 2 else db), z))
+
+        def to_inner():
+            return remote(tot.at[at], zin.at[0, at], z_send.at[k, 0], z_recv.at[k, 0], (f, 1 + z // 3))
+
+        def across():
+            return remote(tot.at[at], zin.at[1, at], z_send.at[k, 0], z_recv.at[k, 1], (f, 3 - z))
+
+        def to_outer():
+            return remote(out.at[at], zin.at[1, at], z_send.at[k, 1], z_recv.at[k, 1], (f, 3 * (z - 1)))
+
+        def merge(m):
+            if copied:
+                load(m).wait()
+            swap(m).wait_recv()
+            h = held(m)
+            h[...] = h[...] + yours[m, at]
+
+        def s0():
+            for m in range(4):
+                swap(m).start()
+                if copied:
+                    load(m).start()
+
+        def s1():
+            for m in range(2):
+                merge(m)
+                hop(m).start()
+
+        def s2():
+            merge(2)
+            hop(0).wait_recv()
+            h = held(2)
+            h[...] = h[...] + came[0, at]
+            hop(2).start()
+            merge(3)
+
+        def s3():
+            hop(1).wait_recv()
+            hop(2).wait_recv()
+            total = held(3)[...].astype(F32) + came[1, at].astype(F32) + came[2, at].astype(F32)
+            tot[at] = total.astype(tot.dtype)
+
+            @pl.when(outer)
+            def _():
+                to_inner().start()
+
+        def s4():
+            @pl.when(inner)
+            def _():
+                to_inner().wait_recv()
+                tot[at] = tot[at] + zin[0, at]
+                across().start()
+
+        def s5():
+            @pl.when(inner)
+            def _():
+                across().wait_recv()
+                out[at] = tot[at] + zin[1, at]
+                to_outer().start()
+
+        def s6():
+            @pl.when(outer)
+            def _():
+                to_outer().wait_recv()
+                out[at] = zin[1, at]
+                to_inner().wait_send()
+
+            @pl.when(inner)
+            def _():
+                across().wait_send()
+                to_outer().wait_send()
+
+            for m in range(4):
+                swap(m).wait_send()
+            for i in range(3):
+                hop(i).wait_send()
+
+        return [s0, s1, s2, s3, s4, s5, s6]
+
+    return [steps(k, lo, size) for k, (lo, size) in enumerate(cuts)]
+
+
+def drain(every, done):
+    count = len(every)
+    for t in range(count + 6):
+        for s in range(6, 0, -1):
+            k = t - s
+            if 0 <= k < count and (k, s) not in done:
+                every[k][s]()
+
+
+def even_cuts(rows, parts):
+    size = rows // parts // 16 * 16
+    cuts = [(i * size, size) for i in range(parts - 1)]
+    return cuts + [((parts - 1) * size, rows - (parts - 1) * size)]
+
+
+def relay_partner(f, z, turn):
+    return f - f % 2 + z // 2, 2 * (f % 2) + (z + turn) % 2
+
+
+def greet(relay):
+    f, z, mate, da, db = places()
+    barrier = pltpu.get_barrier_semaphore()
+
+    def signal(group, place):
+        pl.semaphore_signal(barrier, inc=1, device_id=(group, place), device_id_type=MESH)
+
+    for other in (mate, f + da, f + db):
+        signal(other, z)
+
+    @pl.when(z > 0)
+    def _():
+        signal(f, z - 1)
+
+    @pl.when(z < 3)
+    def _():
+        signal(f, z + 1)
+
+    if relay:
+        signal(*relay_partner(f, z, 1))
+
+        @pl.when(z // 2 != f % 2)
+        def _():
+            signal(*relay_partner(f, z, 0))
+
+    away = z // 2 - f % 2
+    count = 4 + (z + 2) // 3 - z // 3
+    pl.semaphore_wait(barrier, count + 1 + away * away if relay else count)
+
+
+def relay_steps(src, out, sems):
+    f, z, _mate, _da, _db = places()
+    here = z // 2 == f % 2
+
+    def copy(turn):
+        return pltpu.make_async_remote_copy(
+            src_ref=src.at[turn], dst_ref=out.at[z % 2], send_sem=sems.at[turn], recv_sem=sems.at[2 + turn],
+            device_id=relay_partner(f, z, turn), device_id_type=MESH)
+
+    def local():
+        return pltpu.make_async_copy(src.at[0], out.at[z % 2], sems.at[0])
+
+    def start():
+        copy(1).start()
+
+        @pl.when(here)
+        def _():
+            local().start()
+
+        @pl.when(jnp.logical_not(here))
+        def _():
+            copy(0).start()
+
+    def wait():
+        copy(1).wait()
+
+        @pl.when(here)
+        def _():
+            local().wait()
+
+        @pl.when(jnp.logical_not(here))
+        def _():
+            copy(0).wait()
+
+    return start, wait
+
+
+def att_bwd_kernel(cuts, slots, q_ref, ko_ref, kp_ref, vo_ref, vp_ref, bias_ref, st_ref, do_ref, o_ref, mixed_ref, s0, s1, s2,
+                   dqkv_ref, got_ref, back_ref, r0, r1, r2,
+                   kbuf, vbuf, qx, dox, dkv, kv_send, kv_recv, relay_sems, *scratch):
     step = pl.program_id(0)
+    last = pl.num_programs(0) - 1
+    rows = q_ref.shape[0]
+    f, z, mate, da, db = places()
+    every = []
+    for i, (src, out) in enumerate(((s0, r0), (s1, r1), (s2, r2))):
+        every += reduce_steps(src, out, scratch[REDUCE_REFS_COPIED * i:REDUCE_REFS_COPIED * (i + 1)], cuts[i])
+    relay_start, relay_wait = relay_steps(mixed_ref, back_ref, relay_sems)
+
+    def give(i):
+        cols = pl.ds(i * 128 if isinstance(i, int) else pl.multiple_of(i * 128, 128), 128)
+        return pltpu.make_async_remote_copy(
+            src_ref=dkv.at[i % 2, :, pl.ds(rows, rows)], dst_ref=got_ref.at[:, :, cols],
+            send_sem=kv_send.at[i % 2], recv_sem=kv_recv.at[i], device_id=(mate, z), device_id_type=MESH)
+
     @pl.when(step == 0)
     def _():
-        nt[...] = n_ref[...].T
+        greet(True)
+        for c in every:
+            c[0]()
+        relay_start()
+        kbuf[:, 128:] = bias_ref[...]
+        lane = lax.broadcasted_iota(jnp.int32, (2 * rows, 128), 1)
+        vbuf[:, 128:] = (lane < 3).astype(BF)
+
+    def hook(half):
+        for at, todo in slots.items():
+            if at % 2 == half:
+                @pl.when(step == at // 2)
+                def _(todo=todo):
+                    for k, s in todo:
+                        every[k][s]()
+
+    @pl.when(step >= 2)
+    def _():
+        give(step - 2).wait_send()
+
+    hook(0)
+    kbuf[:rows, :128] = ko_ref[...]
+    kbuf[rows:, :128] = kp_ref[...]
+    vbuf[:rows, :128] = vo_ref[...]
+    vbuf[rows:, :128] = vp_ref[...]
+    lane = lax.broadcasted_iota(jnp.int32, (rows, 128), 1)
+    low = lane < 64
+    q = q_ref[...]
+    do = do_ref[...]
+    prod = do.astype(F32) * o_ref[...].astype(F32)
+    for h in range(2):
+        keep = low if h == 0 else jnp.logical_not(low)
+        qx[h, :, :128] = jnp.where(keep, q, jnp.zeros_like(q))
+        qx[h, :, 128:] = st_ref[h]
+        dox[h, :, :128] = jnp.where(keep, do, jnp.zeros_like(do))
+        total = -jnp.sum(jnp.where(keep, prod, 0.0), axis=-1, keepdims=True)
+        hi = total.astype(BF).astype(F32)
+        mid = (total - hi).astype(BF).astype(F32)
+        lo = total - hi - mid
+        piece = jnp.where(lane == 0, hi, jnp.where(lane == 1, mid, jnp.where(lane == 2, lo, 0.0)))
+        dox[h, :, 128:] = piece.astype(BF)
+    dqs = [None, None]
+    for part in range(2):
+        if part == 1:
+            hook(1)
+        start = part * rows
+        dk = None
+        dv = None
+        kb = kbuf[start:start + rows, :]
+        vb = vbuf[start:start + rows, :]
+        for h in range(2):
+            s = dotf(kb, qx[h], NT)
+            dp = dotf(vb, dox[h], NT)
+            p = jnp.exp(s)
+            ds = (p * dp).astype(BF)
+            p_low = p.astype(BF)
+            dv_h = dotf(p_low, dox[h, :, :128], NN)
+            dk_h = dotf(ds, qx[h, :, :128], NN)
+            dv = dv_h if dv is None else dv + dv_h
+            dk = dk_h if dk is None else dk + dk_h
+            dq_h = dotf(kb[:, :128], ds, TN)
+            dqs[h] = dq_h if dqs[h] is None else dqs[h] + dq_h
+        dkv[step % 2, 0, start:start + rows, :] = dk.astype(BF)
+        dkv[step % 2, 1, start:start + rows, :] = dv.astype(BF)
+    dqs = [d.T for d in dqs]
+    dqkv_ref[0] = (jnp.where(low, dqs[0], dqs[1]) * 0.125).astype(BF)
+    dqkv_ref[1] = dkv[step % 2, 0, :rows, :]
+    dqkv_ref[2] = dkv[step % 2, 1, :rows, :]
+    give(step).start()
+
+    @pl.when(step == last)
+    def _():
+        drain(every, {(k, s) for todo in slots.values() for k, s in todo})
+        give(step - 1).wait_send()
+        give(step).wait_send()
+        for i in range(kv_recv.shape[0]):
+            give(i).wait_recv()
+        relay_wait()
+
+
+def att_bwd(q, kv_own, kv_other, bias, st, do, o, mixed, sums):
+    rows, width = q.shape
+    pairs = width // 128
+    blk = pl.BlockSpec((rows, 128), lambda i: (0, i))
+    blk2 = pl.BlockSpec((rows, 128), lambda i: (0, i + pairs))
+    hbm = pl.BlockSpec(memory_space=pltpu.HBM)
+    parts = (4, 1, 1)
+    cuts = [even_cuts(v.shape[1], p) for v, p in zip(sums, parts)]
+    scratch = []
+    for v, p in zip(sums, parts):
+        scratch += reduce_scratch(v.shape[1], v.shape[2], p, v.dtype)
+    whole = lambda v: pl.BlockSpec(v.shape[1:], lambda i: (0,) * (v.ndim - 1))
+    return pl.pallas_call(
+        functools.partial(att_bwd_kernel, cuts, BWD_SLOTS),
+        grid=(pairs,),
+        in_specs=[blk, blk, blk, blk2, blk2,
+            pl.BlockSpec((2 * rows, 128), lambda i: (0, 0)),
+            pl.BlockSpec((2, rows, 128), lambda i: (i, 0, 0)), blk, blk, hbm, hbm, hbm, hbm],
+        out_specs=[pl.BlockSpec((3, rows, 128), lambda i: (0, 0, i)), hbm, hbm] + [whole(v) for v in sums],
+        out_shape=[jax.ShapeDtypeStruct((3, rows, width), BF), jax.ShapeDtypeStruct((2, rows, width), BF), jax.ShapeDtypeStruct(mixed.shape, BF)]
+        + [jax.ShapeDtypeStruct(v.shape[1:], v.dtype) for v in sums],
+        scratch_shapes=[pltpu.VMEM((2 * rows, 256), BF), pltpu.VMEM((2 * rows, 256), BF),
+            pltpu.VMEM((2, rows, 256), BF), pltpu.VMEM((2, rows, 256), BF), pltpu.VMEM((2, 2, 2 * rows, 128), BF),
+            pltpu.SemaphoreType.DMA((2,)), pltpu.SemaphoreType.DMA((pairs,)), pltpu.SemaphoreType.DMA((4,))] + scratch,
+        compiler_params=pltpu.CompilerParams(vmem_limit_bytes=62 * 2**20, collective_id=1, has_side_effects=True),
+        name="att_bwd",
+    )(q, kv_own, kv_other, kv_own, kv_other, bias, st, do, o, mixed, *sums)
+
+
+BWD_SLOTS = {
+    1: [(0, 1)],
+    2: [(1, 1)],
+    3: [(0, 2)],
+    4: [(2, 1)],
+    5: [(1, 2), (0, 3)],
+    6: [(3, 1)],
+    7: [(0, 4), (2, 2)],
+    8: [(1, 3), (4, 1), (5, 1)],
+    9: [(0, 5), (1, 4)],
+    10: [(3, 2), (2, 3)],
+    11: [(1, 5), (0, 6)],
+    12: [(2, 4), (4, 2), (5, 2)],
+    13: [(3, 3)],
+    14: [(1, 6), (2, 5), (4, 3), (5, 3)],
+    15: [(3, 4)],
+}
+
+
+def qback_kernel(cuts, half, dy_ref, got_ref, x_ref, nt_ref, gmid_ref, vec_ref, w_ref, s0,
+                 back_ref, r0, rq, rs,
+                 gn, dw, gx, small, relay_sems, *scratch):
+    step = pl.program_id(0)
+    groups, part = dw.shape[1:3]
+    every = list(reduce_steps(s0, r0, scratch[:REDUCE_REFS_COPIED], cuts[0]))
+    for i in range(4):
+        at = REDUCE_REFS_COPIED + REDUCE_REFS * i
+        refs = scratch[at:at + REDUCE_REFS]
+        if i < 3:
+            every += reduce_steps(dw.at[i], rq.at[i], refs, [(0, part)], False)
+        else:
+            every += reduce_steps(small, rs, refs, [(0, small.shape[1])], False)
+    fixed = len(cuts[0])
+    relay_start, relay_wait = relay_steps(gx, back_ref, relay_sems)
+
+    def put(row, v):
+        for i in range(groups):
+            small[i, row:row + 1, :] = v[:, i * part:(i + 1) * part]
+
+    col = lambda v: jnp.sum(v, axis=0, keepdims=True)
+
+    @pl.when(step == 0)
+    def _():
+        greet(True)
+        for c in every[:fixed]:
+            c[0]()
         gn[...] = jnp.zeros_like(gn)
-    def do(y):
-        dw_ref[...] = dotf(nt[...], y, NN).astype(BF)
+        small[...] = jnp.zeros_like(small)
+
+    def do(i, y):
+        dw[i] = dotf(nt_ref[...], y, NN).astype(BF).reshape(dw.shape[1:])
+        every[fixed + i][0]()
         gn[...] += dotf(y, w_ref[...], NT)
-        return jnp.sum(y.astype(F32), axis=0, keepdims=True)
+
     @pl.when(step == 0)
     def _():
-        small_ref[0:1, :] = do(dq_ref[...])
+        y = dy_ref[0]
+        put(0, col(y.astype(F32)))
+        do(0, y)
+        for k, s in QBACK_SLOTS[0]:
+            every[k][s]()
+
     @pl.when(step == 1)
     def _():
-        do((dko_ref[...].astype(F32) + dkr_ref[...].astype(F32)).astype(BF))
+        do(1, (dy_ref[0].astype(F32) + got_ref[0].astype(F32)).astype(BF))
+        for k, s in QBACK_SLOTS[1]:
+            every[k][s]()
+
     @pl.when(step == 2)
     def _():
-        small_ref[1:2, :] = do((dvo_ref[...].astype(F32) + dvr_ref[...].astype(F32)).astype(BF))
+        y = (dy_ref[0].astype(F32) + got_ref[0].astype(F32)).astype(BF)
+        put(1, col(y.astype(F32)))
+        do(2, y)
         z, r = norm_parts(x_ref[...].astype(F32))
         g = gn[...]
-        small_ref[2:3, :] = jnp.sum(g * z, axis=0, keepdims=True)
-        small_ref[3:4, :] = jnp.sum(g, axis=0, keepdims=True)
-        gx_ref[...] = (gmid_ref[...] + norm_back(z, r, g, vec_ref[0:1, :])).astype(BF)
-
-def qback(dq, dko, dvo, dkr, dvr, x, n, gmid, vec, w):
+        put(2, col(g * z))
+        put(3, col(g))
+        every[fixed + 3][0]()
+        res = (gmid_ref[...] + norm_back(z, r, g, vec_ref[0:1, :])).astype(BF)
+        gx[0, :half] = res[:half]
+        gx[1, :half] = res[half:]
+        gx[:, half:] = jnp.zeros_like(gx[:, half:])
+        relay_start()
+        drain(every, set(QBACK_SLOTS[0] + QBACK_SLOTS[1]))
+        relay_wait()
+
+
+QBACK_SLOTS = ([(0, 1), (1, 1)], [(0, 2), (2, 1), (1, 2), (0, 3)])
+
+
+def qback(dy, got, x, nt, gmid, vec, w, dw1):
     rows, width = x.shape
+    groups = dw1.shape[0]
+    part = width // groups
+    once = pl.Buffered(1)
     full = lambda s: pl.BlockSpec(s, lambda j: (0,) * len(s))
+    keep = lambda s: pl.BlockSpec(s, lambda j: (0,) * len(s), pipeline_mode=once)
+    hbm = pl.BlockSpec(memory_space=pltpu.HBM)
     sd = jax.ShapeDtypeStruct
-    f = full((rows, width))
-    return pl.pallas_call(qback_kernel, grid=(3,),
-        in_specs=[f] * 8 + [full((8, width)), pl.BlockSpec((width, width), lambda j: (0, j))],
-        out_specs=[pl.BlockSpec((width, width), lambda j: (0, j)), f, full((8, width))],
-        out_shape=[sd((width, 3 * width), BF), sd((rows, width), BF), sd((8, width), F32)],
-        scratch_shapes=[pltpu.VMEM((width, rows), BF), pltpu.VMEM((rows, width), F32)],
-        compiler_params=pltpu.CompilerParams(vmem_limit_bytes=60 * 2**20), name="qback")(dq, dko, dvo, dkr, dvr, x, n, gmid, vec, w)
+    cuts = [even_cuts(dw1.shape[1], 4)]
+    scratch = reduce_scratch(dw1.shape[1], dw1.shape[2], 4, BF)
+    for _ in range(3):
+        scratch += reduce_scratch(part, width, 1, BF, False)
+    scratch += reduce_scratch(8, part, 1, F32, False)
+    pad = (rows // 2 + 15) // 16 * 16
+    return pl.pallas_call(functools.partial(qback_kernel, cuts, rows // 2), grid=(3,),
+        in_specs=[pl.BlockSpec((1, rows, width), lambda j: (j, 0, 0)), pl.BlockSpec((1, rows, width), lambda j: (jnp.maximum(j - 1, 0), 0, 0)),
+            keep((rows, width)), keep((width, rows)), keep((rows, width)), full((8, width)), pl.BlockSpec((width, width), lambda j: (0, j)), hbm],
+        out_specs=[hbm, full(dw1.shape[1:]), full((3, part, width)), full((8, part))],
+        out_shape=[sd((2, pad, width), BF), sd(dw1.shape[1:], BF), sd((3, part, width), BF), sd((8, part), F32)],
+        scratch_shapes=[pltpu.VMEM((rows, width), F32), pltpu.VMEM((3, groups, part, width), BF),
+            pltpu.VMEM((2, pad, width), BF), pltpu.VMEM((groups, 8, part), F32), pltpu.SemaphoreType.DMA((4,))] + scratch,
+        compiler_params=pltpu.CompilerParams(vmem_limit_bytes=63 * 2**20, collective_id=2, has_side_effects=True), name="qback")(
+            dy, got, x, nt, gmid, vec, w, dw1)
 
 
 def relayout_pairs(groups, seq_count, turn):
@@ -697,7 +1070,6 @@
     core = group % 2
     turns = range(2)
     pairs = [relayout_pairs(groups, seq_count, turn) for turn in turns]
-    back = [[(b, a) for a, b in pair] for pair in pairs]
     swap = [(f, f ^ 1) for f in range(groups)]
 
     def spread(block):
@@ -706,11 +1078,6 @@
             sent = lax.dynamic_index_in_dim(block, (place + turn) % 2, 0, keepdims=False)
             parts.append(lax.ppermute(sent, AXES, pairs[turn]))
         return jnp.concatenate(parts, axis=0)
-
-    def collect(block):
-        got = [lax.ppermute(block[turn * tok_here : (turn + 1) * tok_here], AXES, back[turn]) for turn in turns]
-        even = place % 2 == 0
-        return jnp.stack([jnp.where(even, got[0], got[1]), jnp.where(even, got[1], got[0])])
 
     small = jnp.concatenate(
         [
@@ -746,47 +1113,26 @@
     bias_all = jnp.concatenate([bias_q, zero, bias_v], axis=1)
 
     wq = lax.all_gather(qkv_weight, "fsdp", axis=0, tiled=True)
-    normed, q, kv = qkv(x, vec1, wq, bias_all)
+    normed_t, q, kv = qkv(x, vec1, wq, bias_all)
     kv_other = lax.ppermute(kv, "fsdp", swap)
     cot = spread(cotangent)
     wp = lax.all_gather(proj_weight, "fsdp", axis=0, tiled=True)
     w1 = lax.all_gather(fc1_weight, "fsdp", axis=0, tiled=True)
     w2 = lax.all_gather(fc2_weight, "fsdp", axis=0, tiled=True)
     attended, stats = att_fwd(q, kv, kv_other, mask, FWD_BLOCKS(rows))
-    mixed, grad_mid, grad_att, dwp, dw1, dw2, small2, grad_b1 = mlp(attended, x, cot, live, vec2, wp, w1, bias_1, w2)
-    mixed_out = collect(mixed)
-    scatter = lambda v: lax.psum_scatter(v, "fsdp", scatter_dimension=0, tiled=True)
-    dw2_part = scatter(dw2)
-    dw1_part = scatter(dw1)
-    dwp_part = scatter(dwp)
-    dq, dko, dkp, dvo, dvp = att_bwd(q, kv, kv_other, mask, stats, grad_att, attended, (rows, rows))
-    dkr = lax.ppermute(dkp, "fsdp", swap)
-    dvr = lax.ppermute(dvp, "fsdp", swap)
-    dwq, grad_x, small1 = qback(dq, dko, dvo, dkr, dvr, x, normed, grad_mid, vec1, wq)
-    input_grad = collect(grad_x).astype(F32)
-    dwq_part = scatter(dwq)
-    totals = lax.psum((dw2_part, dw1_part, dwp_part), "seq")
-    total_q = lax.psum(dwq_part, "seq")
-    image = jnp.arange(groups * images_here, dtype=jnp.int32)
-    mine = image == (column * 2 + place // 2) * images_here + place % 2
-    squares = jnp.sum(small2[8:13], axis=1)
-    squares = jnp.where(mine[:, None], squares[None, :], 0.0)
-    sums = jnp.concatenate(
-        [
-            small1[2], small1[3], small1[0], small1[1], small2[5], small2[4], small2[2], small2[3],
-            small2[1], small2[0], grad_b1[0], squares.reshape(-1),
-        ]
-    )
-    sums = lax.psum(sums, AXES)
-    grads = [lax.dynamic_slice(sums, (i * width + group * part,), (part,)) for i in range(10)]
-    g_gain1, g_shift1, g_bq, g_bv, g_bp, g_scale1, g_gain2, g_shift2, g_b2, g_scale2 = grads
-    g_b1 = lax.dynamic_slice(sums, (10 * width + group * ff_part,), (ff_part,))
-    squares = sums[10 * width + groups * ff_part :].reshape(groups * images_here, 5)
-    squares = lax.dynamic_slice(squares, (group * images_here, 0), (images_here, 5))
+    mixed, grad_mid, grad_att, dwp, dw1, dw2, small2 = mlp(attended, x, cot, live, vec2, wp, w1, bias_1, w2, groups)
+    cut = lambda v: v.reshape(groups, v.shape[0] // groups, v.shape[1])
+    dqkv, got, mixed_out, total_2, total_p, sums2 = att_bwd(
+        q, kv, kv_other, mask, stats, grad_att, attended, mixed, (cut(dw2), cut(dwp), small2)
+    )
+    grad_x, total_1, total_q, sums1 = qback(dqkv, got, x, normed_t, grad_mid, vec1, wq, cut(dw1))
+    total_q = jnp.concatenate([total_q[0], total_q[1], total_q[2]], axis=1).astype(F32)
+    squares = sums2[14, : images_here * 5].reshape(images_here, 5)
     rms = jnp.sqrt(squares / (valid_len.astype(F32)[:, None] * width))
     return (
-        mixed_out, input_grad, rms, g_gain1, g_shift1, total_q.astype(F32), g_bq, g_bv, totals[2].astype(F32), g_bp,
-        g_scale1, g_gain2, g_shift2, totals[1].astype(F32), g_b1, totals[0].astype(F32), g_b2, g_scale2,
+        mixed_out[:, :tok_here], grad_x[:, :tok_here].astype(F32), rms, sums1[2], sums1[3], total_q, sums1[0], sums1[1],
+        total_p.astype(F32), sums2[5], sums2[4], sums2[2], sums2[3], total_1.astype(F32), sums2[10:14].reshape(-1),
+        total_2.astype(F32), sums2[1], sums2[0],
     )
 
 
@@ -837,7 +1183,7 @@
         P("fsdp"),
     )
     seq_count = mesh.shape["seq"]
-    paired = seq_count == 4 and mesh.shape["fsdp"] % 2 == 0
+    paired = seq_count == 4 and mesh.shape["fsdp"] == 8
     return jax.shard_map(
         fast_device if paired else generic_device, mesh=mesh, in_specs=in_specs, out_specs=out_specs, check_vma=False
     )

time: 726 us -> 508 us (0.70)
  waiting for transfers between devices: 341 us -> 92.9 us
  Pallas kernels: 184 us -> 319 us
  blocking collectives: 129 us -> 27.4 us
  starting transfers between devices: 18.5 us -> 7.94 us
    reduce_scatter x4 -> x0, waiting for transfers between devices: 205 us -> none  [fast_device(): lax.psum_scatter(v, 'fsdp', scatter_dimension=0, tiled=True)]
    pallas_call x2, Pallas kernels: 69.2 us -> 205 us  [the longest x1 118 us: qback(): pl.pallas_call(functools.partial(qback_kernel, cuts, rows // 2), grid=(3,...]
    psum x1 -> x0, blocking collectives: 102 us -> none  [fast_device(): sums = lax.psum(sums, AXES)]
    psum x1 -> x0, waiting for transfers between devices: 40.2 us -> none  [fast_device(): total_q = lax.psum(dwq_part, 'seq')]
    all_gather x1, waiting for transfers between devices: 6.34 us -> 20.8 us  [fast_device(): w1 = lax.all_gather(fc1_weight, 'fsdp', axis=0, tiled=True)]
    ppermute x4, waiting for transfers between devices: 12.9 us -> 2.24 us  [spread(): parts.append(lax.ppermute(sent, AXES, pairs[turn]))]
  transfers between devices with their start and end apart: 20 -> 9, of which waited for: 10 -> 4; matrix products, arithmetic and copies ran while one was open for 4% -> 4% of each run, Pallas kernels for 15% -> 9%
where the time goes in v2:
time: 508 us; the launch traced here: 500 us
  Pallas kernels  319 us (63%)
  waiting for transfers between devices  92.9 us (18%)
  blocking collectives  27.4 us (5%)
  other arithmetic  19.4 us (4%)
  local copies, waits for them, and re-layouts  18.3 us (4%)
  between operations  15 us (3%)
  starting transfers between devices  7.94 us (2%)
    pallas_call x1, Pallas kernels, qback(): pl.pallas_call(functools.partial(qback_kernel, cuts, rows // 2), grid=(3,...  118 us
    pallas_call x1, Pallas kernels, att_bwd(): pl.pallas_call(functools.partial(att_bwd_kernel, cuts, BWD_SLOTS), grid=(...  87 us
    pallas_call x1, Pallas kernels, mlp(): pl.pallas_call(mlp_kernel, grid=(ff // fc,), in_specs=[full((rows, width)...  72 us
    all_gather x1, waiting for transfers between devices, fast_device(): w2 = lax.all_gather(fc2_weight, 'fsdp', axis=0, tiled=True)  56.2 us
    pallas_call x1, Pallas kernels, att_fwd(): pl.pallas_call(functools.partial(att_fwd_kernel, blocks), grid=(pairs,),...  31.5 us
    unnamed x1, blocking collectives  27.4 us
    all_gather x1, waiting for transfers between devices, fast_device(): w1 = lax.all_gather(fc1_weight, 'fsdp', axis=0, tiled=True)  20.8 us
    all_gather x1, waiting for transfers between devices, fast_device(): wq = lax.all_gather(qkv_weight, 'fsdp', axis=0, tiled=True)  11.1 us
  transfers between devices with their start and end apart: 9, of which 4 were waited for; matrix products, arithmetic and copies ran while one was open for 4% of the time, Pallas kernels for 9%

profile of v2, /device:TPU:0, one launch (start us, length us, event | category | flops | bytes accessed | tf_op | source)
XLA Modules:
  0.0 500.4 jit_solution(7897046060995316859)
XLA Ops:
  10.3 1.5 collective-permute-start
  11.8 3.0 collective-permute-start.1
  16.6 27.4 %all-reduce = bf16[14368]{0:T(1024)(128)(2,1)S(1)} all-reduce(bf16[14368]{0:T(1024)(128)(2,1)S(1)} %dynamic-update-slice), channel_id=2, replica_groups=mesh['fsdp'=8,'seq'=4] {'fsdp'}, use_global_device_ids=true, to_apply=%add | all-reduce | flops 14368 | bytes 57472
  47.3 11.1 %all-gather.6.cloned.1.call-done.w_ref = bf16[1024,3072]{1,0:T(8,128)(2,1)} async-done(((bf16[128,3072]{1,0:T(8,128)(2,1)}), bf16[1024,3072]{1,0:T(8,128)(2,1)}) %all-gather.6.cloned.1.call-update) | async-done | bytes 6291472 | tf_op jit(solution)/shard_map/all_gather | solution.py:1115
  58.4 11.1 %qkv.1 = (bf16[1024,688]{1,0:T(8,128)(2,1)}, bf16[688,1024]{1,0:T(8,128)(2,1)}, bf16[688,2048]{1,0:T(8,128)(2,1)}) custom-call(bf16[688,1024]{1,0:T(8,128)(2,1)} %copy-done.1, f32[8,1024]{1,0:T(8,128)} %maximum_maximum_fusion.vec_ref, bf16[1024,3072]{1,0:T(8,128)(2,1)} %all-gather.6.cloned.1.call-done.w_ref, f32[1,3072]{1,0:T(1,128)} %pad_maximum_fusion.1.b_ref), custom_call_target="tpu_custom_call" | custom-call | tf_op jit(solution)/shard_map/qkv/pallas_call | solution.py:552
  70.7 1.4 collective-permute-start.4
  72.2 1.5 collective-permute-start.3
  79.2 1.6 copy.54.live_ref
  82.2 1.4 concatenate.60.vec_ref
  84.2 1.7 select_convert_fusion.bias_ref
  85.9 2.2 collective-permute-done.4
  88.1 2.5 pad_maximum_fusion.cot_ref
  90.6 1.5 copy-done
  92.1 31.5 %att_fwd.1 = (bf16[688,1024]{1,0:T(8,128)(2,1)}, bf16[16,688,128]{2,1,0:T(8,128)(2,1)}) custom-call(bf16[688,1024]{1,0:T(8,128)(2,1)} %get-tuple-element.40.q_ref, bf16[688,2048]{1,0:T(8,128)(2,1)} %get-tuple-element.41.ko_ref.vo_ref, bf16[688,2048]{1,0:T(8,128)(2,1)} %copy-done, bf16[688,2048]{1,0:T(8,128)(2,1)} %get-tuple-element.41.ko_ref.vo_ref, ...), custom_call_target="tpu_custom_call" | custom-call | tf_op jit(solution)/shard_map/att_fwd/pallas_call | solution.py:393
  123.6 20.8 %all-gather.10.cloned.1.call-done.w1_ref = bf16[1024,4096]{1,0:T(8,128)(2,1)} async-done(((bf16[128,4096]{1,0:T(8,128)(2,1)}), bf16[1024,4096]{1,0:T(8,128)(2,1)}) %all-gather.10.cloned.1.call-update) | async-done | bytes 8388624 | tf_op jit(solution)/shard_map/all_gather | solution.py:1120
  144.4 56.2 %all-gather.12.cloned.1.call-done.w2_ref = bf16[4096,1024]{1,0:T(8,128)(2,1)} async-done(((bf16[512,1024]{1,0:T(8,128)(2,1)}), bf16[4096,1024]{1,0:T(8,128)(2,1)}) %all-gather.12.cloned.1.call-update) | async-done | bytes 8388624 | tf_op jit(solution)/shard_map/all_gather | solution.py:1121
  200.6 72.0 %mlp.1 = (bf16[2,352,1024]{2,1,0:T(8,128)(2,1)}, f32[688,1024]{1,0:T(8,128)}, bf16[688,1024]{1,0:T(8,128)(2,1)}, bf16[1024,1024]{1,0:T(8,128)(2,1)}, bf16[1024,4...) custom-call(bf16[688,1024]{1,0:T(8,128)(2,1)} %get-tuple-element.43.att_ref.o_ref, ...), custom_call_target="tpu_custom_call" | custom-call | tf_op jit(solution)/shard_map/mlp/pallas_call | solution.py:519
  272.7 87.0 %att_bwd.1 = (bf16[3,688,1024]{2,1,0:T(8,128)(2,1)}, bf16[2,688,1024]{2,1,0:T(8,128)(2,1)}, bf16[2,352,1024]{2,1,0:T(8,128)(2,1)}, bf16[512,1024]{1,0:T(8,128)(2...) custom-call(bf16[688,1024]{1,0:T(8,128)(2,1)} %get-tuple-element.40.q_ref, ...), custom_call_target="tpu_custom_call" | custom-call | tf_op jit(solution)/shard_map/att_bwd/pallas_call | solution.py:897
  360.4 1.4 slice_bitcast_fusion.5
  363.1 2.5 slice.107
  365.6 117.9 %qback.1 = (bf16[2,352,1024]{2,1,0:T(8,128)(2,1)}, bf16[128,4096]{1,0:T(8,128)(2,1)}, bf16[3,128,1024]{2,1,0:T(8,128)(2,1)}, f32[8,128]{1,0:T(8,128)}) custom-call(bf16[3,688,1024]{2,1,0:T(8,128)(2,1)} %get-tuple-element.50.dy_ref, bf16[2,688,1024]{2,1,0:T(8,128)(2,1)} %get-tuple-element.51.got_ref, bf16[688,1024]{1,0:T(8,128)(2,1)} %copy-done.1, ...), custom_call_target="tpu_custom_call" | custom-call | tf_op jit(solution)/shard_map/qback/pallas_call | solution.py:1019
  483.5 3.3 slice_convert_fusion
  488.7 1.5 convert_element_type.54
  490.2 1.6 convert_element_type.55
  (104 shorter events, 21.7 us)
Async XLA Ops:
  7.2 51.2 %all-gather.6.cloned.1.call-start = ((), (), s32[]{:S(2)}) async-start(), calls=%async_computation | async-start | bytes 7077888 | tf_op jit(solution)/shard_map/all_gather | solution.py:1115
  7.9 115.7 %all-gather.8.cloned.1.call-start = ((), (), s32[]{:S(2)}) async-start(), calls=%async_computation.1 | async-start | bytes 2359296 | tf_op jit(solution)/shard_map/all_gather | solution.py:1119
  8.7 135.8 %all-gather.10.cloned.1.call-start = ((), (), s32[]{:S(2)}) async-start(), calls=%async_computation.2 | async-start | bytes 9437184 | tf_op jit(solution)/shard_map/all_gather | solution.py:1120
  9.4 191.2 %all-gather.12.cloned.1.call-start = ((), (), s32[]{:S(2)}) async-start(), calls=%async_computation.3 | async-start | bytes 9437184 | tf_op jit(solution)/shard_map/all_gather | solution.py:1121
  10.0 6.0 %copy-start.22 = (s32[2]{0:T(128)S(1)}, s32[2]{0:T(128)}, u32[]{:S(2)}) copy-start(s32[2]{0:T(128)} %param.19) | copy-start | bytes 28
  10.0 6.1 %copy-start.10 = (bf16[512]{0:T(512)(128)(2,1)S(1)}, bf16[512]{0:T(512)(128)(2,1)}, u32[]{:S(2)}) copy-start(bf16[512]{0:T(512)(128)(2,1)} %param.32) | copy-start | bytes 3076
  10.0 6.1 %copy-start.11 = (bf16[128]{0:T(256)(128)(2,1)S(1)}, bf16[128]{0:T(256)(128)(2,1)}, u32[]{:S(2)}) copy-start(bf16[128]{0:T(256)(128)(2,1)} %param.21) | copy-start | bytes 772
  10.0 6.1 %copy-start.12 = (bf16[128]{0:T(256)(128)(2,1)S(1)}, bf16[128]{0:T(256)(128)(2,1)}, u32[]{:S(2)}) copy-start(bf16[128]{0:T(256)(128)(2,1)} %param.22) | copy-start | bytes 772
  10.1 6.1 %copy-start.13 = (bf16[128]{0:T(256)(128)(2,1)S(1)}, bf16[128]{0:T(256)(128)(2,1)}, u32[]{:S(2)}) copy-start(bf16[128]{0:T(256)(128)(2,1)} %param.24) | copy-start | bytes 772
  10.1 6.1 %copy-start.14 = (bf16[128]{0:T(256)(128)(2,1)S(1)}, bf16[128]{0:T(256)(128)(2,1)}, u32[]{:S(2)}) copy-start(bf16[128]{0:T(256)(128)(2,1)} %param.25) | copy-start | bytes 772
  10.1 6.1 %copy-start.15 = (bf16[128]{0:T(256)(128)(2,1)S(1)}, bf16[128]{0:T(256)(128)(2,1)}, u32[]{:S(2)}) copy-start(bf16[128]{0:T(256)(128)(2,1)} %param.27) | copy-start | bytes 772
  10.1 6.1 %copy-start.16 = (bf16[128]{0:T(256)(128)(2,1)S(1)}, bf16[128]{0:T(256)(128)(2,1)}, u32[]{:S(2)}) copy-start(bf16[128]{0:T(256)(128)(2,1)} %param.28) | copy-start | bytes 772
  10.1 6.1 %copy-start.17 = (bf16[128]{0:T(256)(128)(2,1)S(1)}, bf16[128]{0:T(256)(128)(2,1)}, u32[]{:S(2)}) copy-start(bf16[128]{0:T(256)(128)(2,1)} %param.29) | copy-start | bytes 772
  10.1 6.1 %copy-start.18 = (bf16[128]{0:T(256)(128)(2,1)S(1)}, bf16[128]{0:T(256)(128)(2,1)}, u32[]{:S(2)}) copy-start(bf16[128]{0:T(256)(128)(2,1)} %param.30) | copy-start | bytes 772
  10.1 6.1 %copy-start.19 = (bf16[128]{0:T(256)(128)(2,1)S(1)}, bf16[128]{0:T(256)(128)(2,1)}, u32[]{:S(2)}) copy-start(bf16[128]{0:T(256)(128)(2,1)} %param.34) | copy-start | bytes 772
  10.1 6.1 %copy-start.20 = (bf16[128]{0:T(256)(128)(2,1)S(1)}, bf16[128]{0:T(256)(128)(2,1)}, u32[]{:S(2)}) copy-start(bf16[128]{0:T(256)(128)(2,1)} %param.35) | copy-start | bytes 772
  10.3 35.7 %collective-permute-start = (bf16[344,1024]{1,0:T(8,128)(2,1)S(1)}, bf16[344,1024]{1,0:T(8,128)(2,1)}, u32[]{:S(2)}, u32[]{:S(2)}) collective-permute-start(bf16[344,1024]{1,0:T(8,128)(2,1)S(1)} %get-tuple-element.65), channel_id=1, source_target_pairs={{0,0},{1,1},{2,4},{3,5},{4,2},{5,3},{6,6},{7,7},{8,8},{9,9},{10,12... | collective-permute-start | bytes 2113544 | tf_op jit(solution)/shard_map/ppermute | solution.py:1079
  11.8 35.4 %collective-permute-start.1 = (bf16[344,1024]{1,0:T(8,128)(2,1)S(1)}, bf16[344,1024]{1,0:T(8,128)(2,1)S(1)}, u32[]{:S(2)}, u32[]{:S(2)}) collective-permute-start(bf16[344,1024]{1,0:T(8,128)(2,1)S(1)} %get-tuple-element.64), channel_id=1, source_target_pairs={{0,1},{1,0},{2,5},{3,4},{4,3},{5,2},{6,7},{7,6},{8,9},{9,8},{10,13... | collective-permute-start | bytes 2113544 | tf_op jit(solution)/shard_map/ppermute | solution.py:1079
  44.0 25.4 %copy-start.8 = (f32[8,1796]{1,0:T(8,128)}, f32[8,1796]{1,0:T(8,128)S(1)}, u32[]{:S(2)}) copy-start(f32[8,1796]{1,0:T(8,128)S(1)} %reshape.171) | copy-start | bytes 172420
  47.2 11.1 %copy-start.1 = (bf16[688,1024]{1,0:T(8,128)(2,1)}, bf16[688,1024]{1,0:T(8,128)(2,1)S(1)}, u32[]{:S(2)}) copy-start(bf16[688,1024]{1,0:T(8,128)(2,1)S(1)} %constant_dynamic-update-slice_fusion.x_ref) | copy-start | bytes 4227076
  58.4 11.4 %copy-start.3 = (bf16[2,344,1024]{2,1,0:T(8,128)(2,1)S(1)}, bf16[2,344,1024]{2,1,0:T(8,128)(2,1)}, u32[]{:S(2)}) copy-start(bf16[2,344,1024]{2,1,0:T(8,128)(2,1)} %param.20) | copy-start | bytes 4227076
  69.4 21.2 %collective-permute-start.2 = (bf16[688,2048]{1,0:T(8,128)(2,1)}, bf16[688,2048]{1,0:T(8,128)(2,1)S(1)}, u32[]{:S(2)}, u32[]{:S(2)}) collective-permute-start(bf16[688,2048]{1,0:T(8,128)(2,1)} %get-tuple-element.41.ko_ref.vo_ref), channel_id=1, source_target_pairs={{0,4},{4,0},{8,12},{12,8},{16,20},{20,16},{24,28},{28,24},{1,5},{5... | collective-permute-start | bytes 8454152 | tf_op jit(solution)/shard_map/ppermute | solution.py:1117
  70.7 17.4 %collective-permute-start.4 = (bf16[344,1024]{1,0:T(8,128)(2,1)}, bf16[344,1024]{1,0:T(8,128)(2,1)}, u32[]{:S(2)}, u32[]{:S(2)}) collective-permute-start(bf16[344,1024]{1,0:T(8,128)(2,1)} %get-tuple-element.63), channel_id=1, source_target_pairs={{0,1},{1,0},{2,5},{3,4},{4,3},{5,2},{6,7},{7,6},{8,9},{9,8},{10,13... | collective-permute-start | bytes 2113544 | tf_op jit(solution)/shard_map/ppermute | solution.py:1079
  72.2 15.9 %collective-permute-start.3 = (bf16[344,1024]{1,0:T(8,128)(2,1)S(1)}, bf16[344,1024]{1,0:T(8,128)(2,1)}, u32[]{:S(2)}, u32[]{:S(2)}) collective-permute-start(bf16[344,1024]{1,0:T(8,128)(2,1)S(1)} %get-tuple-element.62), channel_id=1, source_target_pairs={{0,0},{1,1},{2,4},{3,5},{4,2},{5,3},{6,6},{7,7},{8,8},{9,9},{10,12... | collective-permute-start | bytes 2113544 | tf_op jit(solution)/shard_map/ppermute | solution.py:1079
  (10 other events, 26.8 us)
Sparse Core Ops, SparseCore 0:
  9.9 48.3 all-gather.5
  60.2 27.8 all-gather.7
  90.0 54.3 all-gather.9
  146.2 54.3 all-gather.11
